TPU v7x, 32 devices: a whole 2x2x4 slice. The times are simulated.
32 devices in a mesh: fsdp: 8 (over z, x), tp: 4 (over y, core).
Axes of the slice: x: 2, y: 2, z: 4, core: 2. Of those that a mesh axis runs over, the one named last changes fastest.
Arguments:
- tokens: bfloat16 [16384, 768], P(('fsdp', 'tp')), may hold values from -6 to 6
- segment_ids: int32 [16384], P('fsdp'), may hold values from 0 to 127, never falling along the last dimension, each value on 1 to 512 neighbouring positions
- query_weight: bfloat16 [768, 768], P('fsdp', 'tp'), may hold values from -0.21875 to 0.21875
- key_weight: bfloat16 [768, 768], P('fsdp', 'tp'), may hold values from -0.21875 to 0.21875
- value_weight: bfloat16 [768, 768], P('fsdp', 'tp'), may hold values from -0.21875 to 0.21875
- query_bias: float32 [768], replicated, may hold values from -3 to 3
- value_bias: float32 [768], replicated, may hold values from -3 to 3
- output_weight: bfloat16 [768, 768], P('tp', 'fsdp'), may hold values from -0.625 to 0.625
- output_bias: float32 [768], replicated, may hold values from -3 to 3
- first_gain: float32 [768], replicated, may hold values from 0.1 to 1.9
- first_shift: float32 [768], replicated, may hold values from -3 to 3
- up_weight: bfloat16 [768, 3072], P('fsdp', 'tp'), may hold values from -0.21875 to 0.21875
- up_bias: float32 [3072], replicated, may hold values from -3 to 3
- down_weight: bfloat16 [3072, 768], P('tp', 'fsdp'), may hold values from -0.109375 to 0.109375
- down_bias: float32 [768], replicated, may hold values from -3 to 3
- second_gain: float32 [768], replicated, may hold values from 0.1 to 1.9
- second_shift: float32 [768], replicated, may hold values from -3 to 3
- cotangent: bfloat16 [16384, 768], P(('fsdp', 'tp')), may hold values from -6 to 6
Outputs:
- layer_output: float32 [16384, 768], P(('fsdp', 'tp'))
- input_grad: float32 [16384, 768], P(('fsdp', 'tp'))
- query_weight_grad: float32 [768, 768], P('fsdp', 'tp')
- key_weight_grad: float32 [768, 768], P('fsdp', 'tp')
- value_weight_grad: float32 [768, 768], P('fsdp', 'tp')
- query_bias_grad: float32 [768], P('tp')
- value_bias_grad: float32 [768], P('tp')
- output_weight_grad: float32 [768, 768], P('tp', 'fsdp')
- output_bias_grad: float32 [768], replicated
- first_gain_grad: float32 [768], replicated
- first_shift_grad: float32 [768], replicated
- up_weight_grad: float32 [768, 3072], P('fsdp', 'tp')
- up_bias_grad: float32 [3072], P('tp')
- down_weight_grad: float32 [3072, 768], P('tp', 'fsdp')
- down_bias_grad: float32 [768], replicated
- second_gain_grad: float32 [768], replicated
- second_shift_grad: float32 [768], replicated
Inputs may be any that keep to these rules, and one draw needn't show every extreme that they name: segment_ids never fall along the tokens; each document holds 1 to 512 tokens, and one holds exactly 512.
All inputs are finite; a program needn't handle non-finite values.
Results may differ from a plain program's by a relative error of at most 0.018.
Values may be sent and summed in bfloat16 or wider, within the bound.
No kernel may reach another device: no remote copies, remote signals or barrier semaphores. Data moves between devices by JAX's collectives and lax.ppermute only.
A program may use at most 128 MiB of HBM per device.

v0:
```python
from functools import partial
import math

import jax
import jax.numpy as jnp
from jax import lax
from jax.sharding import PartitionSpec as P

D = 768
HD = 64
FF = 3072
SEQ = 512


def split_up(array, dim, size):
    dims = array.shape
    blocks = array.reshape(*dims[:dim], size, dims[dim] // size, *dims[dim + 1 :])
    return jnp.moveaxis(blocks, dim, 0)


def sent_and_summed(array, axis, dim):
    size = lax.axis_size(axis)
    blocks = lax.all_to_all(split_up(array, dim, size), axis, 0, 0, tiled=True)
    return jnp.sum(blocks.astype(jnp.float32), axis=0)


def side_by_side(arrays, axis, dim, along):
    ends, at = ([], 0)
    for a in arrays[:-1]:
        at += a.shape[along]
        ends.append(at)
    both = jnp.concatenate(arrays, axis=along)
    return tuple(jnp.split(sent_and_summed(both, axis, dim), ends, axis=along))


def inner_rows(former, latter):
    return lax.dot_general(
        former, latter, (((0,), (0,)), ((), ())), preferred_element_type=jnp.float32
    )


def times_trans(former, latter):
    return lax.dot_general(
        former, latter, (((1,), (1,)), ((), ())), preferred_element_type=jnp.float32
    )


def norm_forward(values, norm_gain, norm_shift):
    average = jnp.mean(values, axis=-1, keepdims=True)
    centered = values - average
    inverse = lax.rsqrt(jnp.mean(centered * centered, axis=-1, keepdims=True) + 1e-12)
    normal = centered * inverse
    return (normal * norm_gain + norm_shift, normal, inverse)


def norm_backward(upstream, normal, inverse, norm_gain):
    scaled = upstream * norm_gain
    return inverse * (
        scaled
        - jnp.mean(scaled, axis=-1, keepdims=True)
        - normal * jnp.mean(scaled * normal, axis=-1, keepdims=True)
    )


def masked_scores(queries, keys_all, doc_ids):
    raw_scores = jnp.einsum("qhe,khe->hqk", queries, keys_all, preferred_element_type=jnp.float32)
    raw_scores = raw_scores * (1.0 / math.sqrt(HD))
    same_doc = doc_ids[:, None] == doc_ids[None, :]
    return jnp.where(same_doc[None], raw_scores, -1e30)


def attend(packed):
    queries, keys_all, values_all, doc_ids = packed
    scores = masked_scores(queries, keys_all, doc_ids)
    row_max = jnp.max(scores, axis=-1, keepdims=True)
    exponent = jnp.exp(scores - row_max)
    row_total = jnp.sum(exponent, axis=-1, keepdims=True)
    attention = (exponent / row_total).astype(jnp.bfloat16)
    context = jnp.einsum("hqk,khe->qhe", attention, values_all, preferred_element_type=jnp.float32)
    return (context.astype(jnp.bfloat16), (row_max + jnp.log(row_total))[:, :, 0])


def attend_back(packed):
    queries, keys_all, values_all, doc_ids, log_total, context_grad = packed
    scale_factor = 1.0 / math.sqrt(HD)
    scores = masked_scores(queries, keys_all, doc_ids)
    attention = jnp.exp(scores - log_total[:, :, None])
    prob_grad = jnp.einsum(
        "qhe,khe->hqk", context_grad, values_all, preferred_element_type=jnp.float32
    )
    row_term = jnp.sum(attention * prob_grad, axis=-1, keepdims=True)
    score_grad = (attention * (prob_grad - row_term)).astype(jnp.bfloat16)
    query_grad = jnp.einsum(
        "hqk,khe->qhe", score_grad, keys_all, preferred_element_type=jnp.float32
    )
    key_grad = jnp.einsum("hqk,qhe->khe", score_grad, queries, preferred_element_type=jnp.float32)
    value_grad = jnp.einsum(
        "hqk,qhe->khe",
        attention.astype(jnp.bfloat16),
        context_grad,
        preferred_element_type=jnp.float32,
    )
    return (
        (query_grad * scale_factor).astype(jnp.bfloat16),
        (key_grad * scale_factor).astype(jnp.bfloat16),
        value_grad.astype(jnp.bfloat16),
    )


def shards(
    tokens,
    segment_ids,
    query_weight,
    key_weight,
    value_weight,
    query_bias,
    value_bias,
    output_weight,
    output_bias,
    first_gain,
    first_shift,
    up_weight,
    up_bias,
    down_weight,
    down_bias,
    second_gain,
    second_shift,
    cotangent,
):
    tp_count = lax.axis_size("tp")
    tp_place = lax.axis_index("tp")
    per_device = tokens.shape[0] // SEQ
    fsdp_weights = (
        lax.all_gather(query_weight, "fsdp", axis=0, tiled=True),
        lax.all_gather(key_weight, "fsdp", axis=0, tiled=True),
        lax.all_gather(value_weight, "fsdp", axis=0, tiled=True),
        lax.all_gather(output_weight, "fsdp", axis=1, tiled=True),
        lax.all_gather(up_weight, "fsdp", axis=0, tiled=True),
        lax.all_gather(down_weight, "fsdp", axis=1, tiled=True),
    )
    head_width = D // tp_count
    unit_width = FF // tp_count
    query_add = lax.dynamic_slice_in_dim(query_bias, tp_place * head_width, head_width)
    value_add = lax.dynamic_slice_in_dim(value_bias, tp_place * head_width, head_width)
    up_add = lax.dynamic_slice_in_dim(up_bias, tp_place * unit_width, unit_width)
    query_full, key_full, value_full, output_full, up_full, down_full = fsdp_weights
    head_cols = query_full.shape[1]
    local_heads = head_cols // HD

    def micro_step(totals, inputs):
        seq_tokens, seq_cot, seg_step = inputs
        group_tokens = lax.all_gather(seq_tokens, "tp", axis=0, tiled=True)
        group_rows = group_tokens.shape[0]
        seq_count = group_rows // SEQ

        def heads_view(tensor):
            return tensor.reshape(seq_count, SEQ, local_heads, HD)

        queries = (
            jnp.dot(group_tokens, query_full, preferred_element_type=jnp.float32) + query_add
        ).astype(jnp.bfloat16)
        keys_all = jnp.dot(group_tokens, key_full, preferred_element_type=jnp.float32).astype(
            jnp.bfloat16
        )
        values_all = (
            jnp.dot(group_tokens, value_full, preferred_element_type=jnp.float32) + value_add
        ).astype(jnp.bfloat16)
        context, log_total = lax.map(
            attend, (heads_view(queries), heads_view(keys_all), heads_view(values_all), seg_step)
        )
        context = context.reshape(group_rows, head_cols)
        attn_out = lax.psum_scatter(
            jnp.dot(context, output_full, preferred_element_type=jnp.float32).astype(jnp.bfloat16),
            "tp",
            scatter_dimension=0,
            tiled=True,
        ).astype(jnp.float32)
        first_out, first_normal, first_inverse = norm_forward(
            seq_tokens.astype(jnp.float32) + (attn_out + output_bias), first_gain, first_shift
        )
        first_low = first_out.astype(jnp.bfloat16)
        mid_rows = lax.all_gather(first_low, "tp", axis=0, tiled=True)
        pre_act = jnp.dot(mid_rows, up_full, preferred_element_type=jnp.float32) + up_add
        active = jax.nn.gelu(pre_act, approximate=False).astype(jnp.bfloat16)
        ffn_out = lax.psum_scatter(
            jnp.dot(active, down_full, preferred_element_type=jnp.float32).astype(jnp.bfloat16),
            "tp",
            scatter_dimension=0,
            tiled=True,
        ).astype(jnp.float32)
        layer_output, second_normal, second_inverse = norm_forward(
            first_out + (ffn_out + down_bias), second_gain, second_shift
        )
        upstream = seq_cot.astype(jnp.float32)
        second_gain_grad = jnp.sum(upstream * second_normal, axis=0)
        second_shift_grad = jnp.sum(upstream, axis=0)
        grad_two = norm_backward(upstream, second_normal, second_inverse, second_gain)
        down_bias_grad = jnp.sum(grad_two, axis=0)
        grad_low = grad_two.astype(jnp.bfloat16)
        grad_rows = lax.all_gather(grad_low, "tp", axis=0, tiled=True)
        active_grad = times_trans(grad_rows, down_full)
        gelu_value, gelu_pull = jax.vjp(partial(jax.nn.gelu, approximate=False), pre_act)
        pre_grad = gelu_pull(active_grad)[0].astype(jnp.bfloat16)
        mid_back = lax.psum_scatter(
            times_trans(pre_grad, up_full).astype(jnp.bfloat16),
            "tp",
            scatter_dimension=0,
            tiled=True,
        ).astype(jnp.float32)
        grad_one = grad_two + mid_back
        first_gain_grad = jnp.sum(grad_one * first_normal, axis=0)
        first_shift_grad = jnp.sum(grad_one, axis=0)
        grad_resid = norm_backward(grad_one, first_normal, first_inverse, first_gain)
        output_bias_grad = jnp.sum(grad_resid, axis=0)
        resid_low = grad_resid.astype(jnp.bfloat16)
        resid_rows = lax.all_gather(resid_low, "tp", axis=0, tiled=True)
        context_grad = times_trans(resid_rows, output_full).astype(jnp.bfloat16)
        query_grad, key_grad, value_grad = lax.map(
            attend_back,
            (
                heads_view(queries),
                heads_view(keys_all),
                heads_view(values_all),
                seg_step,
                log_total,
                heads_view(context_grad),
            ),
        )
        query_grad = query_grad.reshape(group_rows, head_cols)
        key_grad = key_grad.reshape(group_rows, head_cols)
        value_grad = value_grad.reshape(group_rows, head_cols)
        input_terms = (
            times_trans(query_grad, query_full)
            + times_trans(key_grad, key_full)
            + times_trans(value_grad, value_full)
        )
        input_back = lax.psum_scatter(
            input_terms.astype(jnp.bfloat16), "tp", scatter_dimension=0, tiled=True
        ).astype(jnp.float32)
        input_grad = grad_resid + input_back
        updates = (
            inner_rows(group_tokens, query_grad),
            inner_rows(group_tokens, key_grad),
            inner_rows(group_tokens, value_grad),
            inner_rows(context, resid_rows),
            inner_rows(mid_rows, pre_grad),
            inner_rows(active, grad_rows),
            jnp.sum(query_grad.astype(jnp.float32), axis=0),
            jnp.sum(value_grad.astype(jnp.float32), axis=0),
            jnp.sum(pre_grad.astype(jnp.float32), axis=0),
            output_bias_grad,
            first_gain_grad,
            first_shift_grad,
            down_bias_grad,
            second_gain_grad,
            second_shift_grad,
        )
        totals = tuple((former + latter for former, latter in zip(totals, updates)))
        return (totals, (layer_output, input_grad))

    initial = (
        tuple((jnp.zeros(weight.shape, jnp.float32) for weight in fsdp_weights))
        + tuple((jnp.zeros(offset.shape, jnp.float32) for offset in (query_add, value_add, up_add)))
        + tuple((jnp.zeros((D,), jnp.float32) for counter in range(6)))
    )
    seg_steps = segment_ids.reshape(tp_count, per_device, SEQ).transpose(1, 0, 2)
    totals, (output_steps, grad_steps) = lax.scan(
        micro_step,
        initial,
        (tokens.reshape(per_device, SEQ, D), cotangent.reshape(per_device, SEQ, D), seg_steps),
    )
    reduced = totals[:9]
    owned_grads = (
        *side_by_side(
            (
                reduced[0].astype(jnp.bfloat16),
                reduced[1].astype(jnp.bfloat16),
                reduced[2].astype(jnp.bfloat16),
            ),
            "fsdp",
            0,
            1,
        ),
        sent_and_summed(reduced[3].astype(jnp.bfloat16), "fsdp", 1),
        sent_and_summed(reduced[4].astype(jnp.bfloat16), "fsdp", 0),
        sent_and_summed(reduced[5].astype(jnp.bfloat16), "fsdp", 1),
    )
    bias_sums = lax.psum((reduced[6], reduced[7], reduced[8]), "fsdp")
    norm_sums = lax.psum(
        (totals[9], totals[10], totals[11], totals[12], totals[13], totals[14]), ("fsdp", "tp")
    )
    return (
        output_steps.reshape(-1, D),
        grad_steps.reshape(-1, D),
        owned_grads[0],
        owned_grads[1],
        owned_grads[2],
        bias_sums[0],
        bias_sums[1],
        owned_grads[3],
        norm_sums[0],
        norm_sums[1],
        norm_sums[2],
        owned_grads[4],
        bias_sums[2],
        owned_grads[5],
        norm_sums[3],
        norm_sums[4],
        norm_sums[5],
    )


def solution(mesh):
    return jax.shard_map(
        shards,
        mesh=mesh,
        in_specs=(
            P(("fsdp", "tp"), None),
            P("fsdp"),
            P("fsdp", "tp"),
            P("fsdp", "tp"),
            P("fsdp", "tp"),
            P(),
            P(),
            P("tp", "fsdp"),
            P(),
            P(),
            P(),
            P("fsdp", "tp"),
            P(),
            P("tp", "fsdp"),
            P(),
            P(),
            P(),
            P(("fsdp", "tp"), None),
        ),
        out_specs=(
            P(("fsdp", "tp"), None),
            P(("fsdp", "tp"), None),
            P("fsdp", "tp"),
            P("fsdp", "tp"),
            P("fsdp", "tp"),
            P("tp"),
            P("tp"),
            P("tp", "fsdp"),
            P(),
            P(),
            P(),
            P("fsdp", "tp"),
            P("tp"),
            P("tp", "fsdp"),
            P(),
            P(),
            P(),
        ),
        check_vma=False,
    )
```

profile of v0, /device:TPU:0, one launch (start us, length us, event | category | flops | bytes accessed | tf_op | source)
XLA Modules:
  0.0 665.6 jit_solution(3971457350717085187)
XLA Ops:
  11.9 35.3 %all_gather.35 = bf16[768,192]{1,0:T(8,128)(2,1)} all-gather(bf16[96,192]{1,0:T(8,128)(2,1)} %param.26), channel_id=1, replica_groups=mesh['fsdp'=8,'tp'=4] {'fsdp'}, dimensions={0}, use_global_device_ids=true | all-gather | bytes 331776 | tf_op jit(solution)/shard_map/all_gather | solution.py:136
  47.2 33.5 %all_gather.36 = bf16[768,192]{1,0:T(8,128)(2,1)} all-gather(bf16[96,192]{1,0:T(8,128)(2,1)} %param.24), channel_id=1, replica_groups=mesh['fsdp'=8,'tp'=4] {'fsdp'}, dimensions={0}, use_global_device_ids=true | all-gather | bytes 331776 | tf_op jit(solution)/shard_map/all_gather | solution.py:134
  80.7 31.4 %all_gather.37 = bf16[768,192]{1,0:T(8,128)(2,1)S(1)} all-gather(bf16[96,192]{1,0:T(8,128)(2,1)} %param.25), channel_id=1, replica_groups=mesh['fsdp'=8,'tp'=4] {'fsdp'}, dimensions={0}, use_global_device_ids=true | all-gather | bytes 331776 | tf_op jit(solution)/shard_map/all_gather | solution.py:135
  112.1 33.0 %all_gather.38 = bf16[192,768]{0,1:T(8,128)(2,1)} all-gather(bf16[192,96]{0,1:T(8,128)(2,1)S(1)} %copy.70), channel_id=1, replica_groups=mesh['fsdp'=8,'tp'=4] {'fsdp'}, dimensions={1}, use_global_device_ids=true | all-gather | bytes 331776 | tf_op jit(solution)/shard_map/all_gather | solution.py:137
  145.1 4.2 fusion.60
  149.2 3.0 reshape.231
  152.2 2.2 copy.66
  154.4 3.1 fusion.61
  157.5 3.0 reshape.232
  160.4 2.2 copy.67
  162.6 2.1 convolution_convert_fusion.4
  164.7 2.4 reshape.233
  167.3 17.4 %while.35 = (s32[]{:T(128)}, bf16[4,512,3,64]{1,3,2,0:T(8,128)(2,1)S(1)}, f32[4,3,512]{2,1,0:T(4,128)}, bf16[4,512,3,64]{1,3,2,0:T(8,128)(2,1)}, s32[4,512]{1,0:...) while((s32[]{:T(128)}, ...), condition=%wide.region_3.4_spmd, body=%wide.region_0.3_spmd.sunk | while | flops 211122688 | bytes 11336281 | solution.py:168
  186.3 2.7 convolution_convert_fusion.2
  190.2 38.0 %reduce-scatter.5.cloned.1.call-done = bf16[512,768]{1,0:T(8,128)(2,1)} async-done(((bf16[2048,768]{1,0:T(8,128)(2,1)}), bf16[512,768]{1,0:T(8,128)(2,1)}) %reduce-scatter.5.cloned.1.call-update) | async-done | bytes 786448 | tf_op jit(solution)/shard_map/while/body/eval_jaxpr/reduce_scatter | solution.py:172
  231.9 2.0 fusion.69
  235.9 27.3 %all-gather.9.cloned.1.call-done = bf16[2048,768]{1,0:T(8,128)(2,1)} async-done(((bf16[512,768]{1,0:T(8,128)(2,1)}), bf16[2048,768]{1,0:T(8,128)(2,1)}) %all-gather.9.cloned.1.call-update) | async-done | bytes 3145744 | tf_op jit(solution)/shard_map/while/body/eval_jaxpr/all_gather | solution.py:182
  263.2 18.9 %multiply_convert_fusion.1 = (bf16[2048,768]{1,0:T(8,128)(2,1)}, f32[2048,768]{1,0:T(8,128)}, f32[2048,768]{1,0:T(8,128)}) fusion(f32[768]{0:T(1024)} %dynamic_slice.52, bf16[2048,768]{1,0:T(8,128)(2,1)} %all-gather.9.cloned.1.call-done, bf16[768,768]{1,0:T(8,128)(2,1)} %all-gather.11.cloned.1.call-done), kind=kOutput, calls=%fused_computation.67 | convolution fusion | flops 2519728128 | bytes 20057088 | tf_op jit(solution)/shard_map/while/body/eval_jaxpr/dot_general | solution.py:183
  282.1 24.9 %all-gather.13.cloned.1.call-done = bf16[768,768]{0,1:T(8,128)(2,1)} async-done(((bf16[768,96]{0,1:T(8,128)(2,1)}), bf16[768,768]{0,1:T(8,128)(2,1)}) %all-gather.13.cloned.1.call-update) | async-done | bytes 1179664 | tf_op jit(solution)/shard_map/all_gather | solution.py:139
  307.0 6.5 convolution_convert_fusion.1
  313.6 36.4 %reduce-scatter.7.cloned.1.call-done = bf16[512,768]{1,0:T(8,128)(2,1)} async-done(((bf16[2048,768]{1,0:T(8,128)(2,1)}), bf16[512,768]{1,0:T(8,128)(2,1)}) %reduce-scatter.7.cloned.1.call-update) | async-done | bytes 786448 | tf_op jit(solution)/shard_map/while/body/eval_jaxpr/reduce_scatter | solution.py:185
  353.6 2.5 fusion.76
  356.4 28.5 %all-gather.15.cloned.1.call-done = bf16[2048,768]{1,0:T(8,128)(2,1)} async-done(((bf16[512,768]{1,0:T(8,128)(2,1)}), bf16[2048,768]{1,0:T(8,128)(2,1)}) %all-gather.15.cloned.1.call-update) | async-done | bytes 3145744 | tf_op jit(solution)/shard_map/while/body/eval_jaxpr/all_gather | solution.py:200
  384.9 11.1 %convert_reduce_fusion = (f32[768]{0:T(1024)}, bf16[2048,768]{1,0:T(8,128)(2,1)S(1)}) fusion(f32[2048,768]{1,0:T(8,128)} %get-tuple-element.334, f32[2048,768]{1,0:T(8,128)} %get-tuple-element.343, f32[768]{0:T(1024)} %dynamic_slice.52, bf16[2048,768]{1,0:T(8,128)(2,1)} %all-gather.15.cloned.1.call-done, bf16[768,768]{0,1:T(8,128)(2,1)} %all-gather.13.cloned.1.call-done), kind=kOutput, calls=%fused_computation.64 | convolution fusion | flops 2442657024 | bytes 20060160 | tf_op jit(solution)/shard_map/while/body/eval_jaxpr/dot_general | solution.py:43
  397.7 4.0 convolution_convert_fusion
  401.8 37.9 %reduce-scatter.9.cloned.1.call-done = bf16[512,768]{1,0:T(8,128)(2,1)} async-done(((bf16[2048,768]{1,0:T(8,128)(2,1)}), bf16[512,768]{1,0:T(8,128)(2,1)}) %reduce-scatter.9.cloned.1.call-update) | async-done | bytes 786448 | tf_op jit(solution)/shard_map/while/body/eval_jaxpr/reduce_scatter | solution.py:204
  439.7 3.4 multiply_reduce_fusion.1
  443.1 2.0 fusion.75
  447.3 6.5 convolution_convert_fusion.5
  453.8 5.5 all-to-all-start.3
  459.4 16.6 %all-gather.17.cloned.1.call-done = bf16[2048,768]{1,0:T(8,128)(2,1)} async-done(((bf16[512,768]{1,0:T(8,128)(2,1)}), bf16[2048,768]{1,0:T(8,128)(2,1)}) %all-gather.17.cloned.1.call-update) | async-done | bytes 3145744 | tf_op jit(solution)/shard_map/while/body/eval_jaxpr/all_gather | solution.py:216
  476.0 3.1 convolution_convert_fusion.3
  481.8 30.0 %while.36 = (s32[]{:T(128)}, bf16[4,512,3,64]{1,3,2,0:T(8,128)(2,1)S(1)}, bf16[4,512,3,64]{1,3,2,0:T(8,128)(2,1)}, bf16[4,512,3,64]{1,3,2,0:T(8,128)(2,1)}, bf16...) while((s32[]{:T(128)}, ...), condition=%wide.region_17.18_spmd, body=%wide.region_15.17_spmd.sunk | while | flops 511146496 | bytes 26127476 | solution.py:218
  514.1 2.0 copy.77
  518.7 2.8 add_convert_fusion
  523.4 5.6 convolution_convert_fusion.6
  529.0 5.8 all-to-all-start.2
  534.8 3.8 convolution_convert_fusion.7
  540.8 2.6 fusion.71
  543.4 20.4 %all-to-all-done.2 = bf16[8,96,768]{2,1,0:T(8,128)(2,1)} async-done(((bf16[8,96,768]{2,1,0:T(8,128)(2,1)}), bf16[8,96,768]{2,1,0:T(8,128)(2,1)}, u32[]{:S(2)}, u32[]{:S(2)}) %all-to-all-start.2) | async-done | bytes 1179680 | tf_op jit(solution)/shard_map/all_to_all | solution.py:23
  563.8 3.6 all-to-all-start.1
  571.9 7.4 %all-to-all-done.1 = bf16[8,192,96]{2,1,0:T(8,128)(2,1)S(1)} async-done(((bf16[8,192,96]{2,1,0:T(8,128)(2,1)}), bf16[8,192,96]{2,1,0:T(8,128)(2,1)S(1)}, u32[]{:S(2)}, u32[]{:S(2)}) %all-to-all-start.1) | async-done | bytes 294944 | tf_op jit(solution)/shard_map/all_to_all | solution.py:23
  580.1 3.6 all-to-all-start
  583.7 2.3 convert_reduce_fusion.2
  586.0 2.2 convert_reduce_fusion.3
  588.2 41.7 %all-reduce = (f32[768]{0:T(1024)}, f32[768]{0:T(1024)}, f32[768]{0:T(1024)}, f32[768]{0:T(1024)}, f32[768]{0:T(1024)}, /*index=5*/f32[768]{0:T(1024)}) all-reduce(f32[768]{0:T(1024)} %get-tuple-element.325, f32[768]{0:T(1024)S(1)} %copy-done.31, f32[768]{0:T(1024)S(1)} %copy-done.32, ...), channel_id=1, replica_groups=mesh['fsdp'=8,'tp'=4] {'fsdp','tp'}, use_global_device_ids=true, to_apply=%region_26.27 | all-reduce | flops 4608 | bytes 36864 | tf_op jit(solution)/shard_map/psum | solution.py:289
  631.6 21.1 %all-reduce.1 = (f32[192]{0:T(256)}, f32[192]{0:T(256)}, f32[768]{0:T(1024)}) all-reduce(f32[192]{0:T(256)S(1)} %reduce_sum.238, f32[192]{0:T(256)S(1)} %reduce_sum.240, f32[768]{0:T(1024)S(1)} %copy-done.34), channel_id=1, replica_groups=mesh['fsdp'=8,'tp'=4] {'fsdp'}, use_global_device_ids=true, to_apply=%region_21.22 | all-reduce | flops 1152 | bytes 9216 | tf_op jit(solution)/shard_map/psum | solution.py:288
  655.4 2.4 convert_add_fusion
  (209 shorter events, 88.3 us)
Async XLA Ops:
  8.0 137.1 %all-gather.7.cloned.1.call-start = ((), (), s32[]{:S(2)}) async-start(), calls=%async_computation.8 | async-start | bytes 3932160 | tf_op jit(solution)/shard_map/while/body/eval_jaxpr/all_gather | solution.py:152
  8.8 219.4 %reduce-scatter.5.cloned.1.call-start = ((), (), s32[]{:S(2)}) async-start(), calls=%async_computation.9 | async-start | bytes 3932160 | tf_op jit(solution)/shard_map/while/body/eval_jaxpr/reduce_scatter | solution.py:172
  112.1 50.5 %copy-start.15 = (bf16[768,192]{1,0:T(8,128)(2,1)}, bf16[768,192]{1,0:T(8,128)(2,1)S(1)}, u32[]{:S(2)}) copy-start(bf16[768,192]{1,0:T(8,128)(2,1)S(1)} %all_gather.37) | copy-start | bytes 884740
  145.1 9.3 %copy-start = (bf16[2048,768]{1,0:T(8,128)(2,1)S(1)}, bf16[2048,768]{1,0:T(8,128)(2,1)}, u32[]{:S(2)}) copy-start(bf16[2048,768]{1,0:T(8,128)(2,1)} %all-gather.7.cloned.1.call-done) | copy-start | bytes 9437188
  164.7 2.6 copy-start.4
  184.6 1.7 copy-start.17
  186.3 41.8 %copy-start.2 = (bf16[512,768]{1,0:T(8,128)(2,1)S(1)}, bf16[512,768]{1,0:T(8,128)(2,1)}, u32[]{:S(2)}) copy-start(bf16[512,768]{1,0:T(8,128)(2,1)} %param.22) | copy-start | bytes 2359300
  186.3 41.8 %copy-start.25 = (f32[768]{0:T(1024)S(1)}, f32[768]{0:T(1024)}, u32[]{:S(2)}) copy-start(f32[768]{0:T(1024)} %param.30) | copy-start | bytes 9220
  189.1 46.8 %all-gather.11.cloned.1.call-start = ((), (), s32[]{:S(2)}) async-start(), calls=%async_computation.11 | async-start | bytes 1327104 | tf_op jit(solution)/shard_map/all_gather | solution.py:138
  189.7 73.5 %all-gather.9.cloned.1.call-start = ((), (), s32[]{:S(2)}) async-start(), calls=%async_computation.10 | async-start | bytes 3932160 | tf_op jit(solution)/shard_map/while/body/eval_jaxpr/all_gather | solution.py:182
  228.2 3.7 copy-start.3
  233.9 73.1 %all-gather.13.cloned.1.call-start = ((), (), s32[]{:S(2)}) async-start(), calls=%async_computation.12 | async-start | bytes 1327104 | tf_op jit(solution)/shard_map/all_gather | solution.py:139
  234.5 115.5 %reduce-scatter.7.cloned.1.call-start = ((), (), s32[]{:S(2)}) async-start(), calls=%async_computation.13 | async-start | bytes 3932160 | tf_op jit(solution)/shard_map/while/body/eval_jaxpr/reduce_scatter | solution.py:185
  313.6 71.3 %all-gather.15.cloned.1.call-start = ((), (), s32[]{:S(2)}) async-start(), calls=%async_computation.14 | async-start | bytes 3932160 | tf_op jit(solution)/shard_map/while/body/eval_jaxpr/all_gather | solution.py:200
  350.0 2.3 copy-start.18
  350.0 2.3 copy-start.28
  350.0 3.6 copy-start.33
  356.2 83.4 %reduce-scatter.9.cloned.1.call-start = ((), (), s32[]{:S(2)}) async-start(), calls=%async_computation.15 | async-start | bytes 3932160 | tf_op jit(solution)/shard_map/while/body/eval_jaxpr/reduce_scatter | solution.py:204
  384.9 12.7 %copy-start.36 = (bf16[768,768]{1,0:T(8,128)(2,1)S(1)}, bf16[768,768]{1,0:T(8,128)(2,1)}, u32[]{:S(2)}) copy-start(bf16[768,768]{1,0:T(8,128)(2,1)} %all-gather.11.cloned.1.call-done) | copy-start | bytes 3538948
  396.0 1.7 copy-start.37
  401.7 74.3 %all-gather.17.cloned.1.call-start = ((), (), s32[]{:S(2)}) async-start(), calls=%async_computation.16 | async-start | bytes 3932160 | tf_op jit(solution)/shard_map/while/body/eval_jaxpr/all_gather | solution.py:216
  439.7 3.4 copy-start.7
  439.7 3.4 copy-start.19
  439.7 3.4 copy-start.26
  445.1 1.1 copy-start.5
  453.8 75.1 %all-to-all-start.3 = ((bf16[8,768,96]{1,2,0:T(8,128)(2,1)}), bf16[8,768,96]{1,2,0:T(8,128)(2,1)}, u32[]{:S(2)}, u32[]{:S(2)}) async-start(bf16[8,768,96]{1,2,0:T(8,128)(2,1)} %bitcast.26), calls=%async_computation.7 | async-start | bytes 2359296 | tf_op jit(solution)/shard_map/all_to_all | solution.py:23
  459.3 196.1 %reduce-scatter.11.cloned.1.call-start = ((), (), s32[]{:S(2)}) async-start(), calls=%async_computation.17 | async-start | bytes 3932160 | tf_op jit(solution)/shard_map/while/body/eval_jaxpr/reduce_scatter | solution.py:237
  511.9 2.2 copy-start.12
  511.9 1.4 copy-start.20
  512.7 4.8 copy-start.9
  513.3 3.0 copy-start.16
  514.1 3.3 copy-start.8
  516.3 2.4 copy-start.10
  516.3 1.3 copy-start.21
  517.6 1.1 copy-start.23
  521.5 1.9 copy-start.35
  529.0 34.8 %all-to-all-start.2 = ((bf16[8,96,768]{2,1,0:T(8,128)(2,1)}), bf16[8,96,768]{2,1,0:T(8,128)(2,1)}, u32[]{:S(2)}, u32[]{:S(2)}) async-start(bf16[8,96,768]{2,1,0:T(8,128)(2,1)} %bitcast.24), calls=%async_computation.6 | async-start | bytes 2359296 | tf_op jit(solution)/shard_map/all_to_all | solution.py:23
  534.8 6.0 copy-start.1
  563.8 15.5 %all-to-all-start.1 = ((bf16[8,192,96]{2,1,0:T(8,128)(2,1)}), bf16[8,192,96]{2,1,0:T(8,128)(2,1)S(1)}, u32[]{:S(2)}, u32[]{:S(2)}) async-start(bf16[8,192,96]{2,1,0:T(8,128)(2,1)} %bitcast.144), calls=%async_computation.5 | async-start | bytes 786432 | tf_op jit(solution)/shard_map/all_to_all | solution.py:23
  567.4 2.0 copy-start.11
  570.5 17.7 %copy-start.29 = (f32[768]{0:T(1024)S(1)}, f32[768]{0:T(1024)}, u32[]{:S(2)}) copy-start(f32[768]{0:T(1024)} %get-tuple-element.276) | copy-start | bytes 9220
  570.5 17.7 %copy-start.30 = (f32[768]{0:T(1024)S(1)}, f32[768]{0:T(1024)}, u32[]{:S(2)}) copy-start(f32[768]{0:T(1024)} %get-tuple-element.281) | copy-start | bytes 9220
  570.5 17.7 %copy-start.31 = (f32[768]{0:T(1024)S(1)}, f32[768]{0:T(1024)}, u32[]{:S(2)}) copy-start(f32[768]{0:T(1024)} %get-tuple-element.273) | copy-start | bytes 9220
  570.5 17.7 %copy-start.32 = (f32[768]{0:T(1024)S(1)}, f32[768]{0:T(1024)}, u32[]{:S(2)}) copy-start(f32[768]{0:T(1024)} %get-tuple-element.278) | copy-start | bytes 9220
  570.5 59.4 %copy-start.13 = (bf16[4,512,3,64]{1,3,2,0:T(8,128)(2,1)S(1)}, bf16[4,512,3,64]{1,3,2,0:T(8,128)(2,1)}, u32[]{:S(2)}) copy-start(bf16[4,512,3,64]{1,3,2,0:T(8,128)(2,1)} %copy-done.12) | copy-start | bytes 2359300
  580.1 74.4 %all-to-all-start = ((bf16[8,96,576]{2,1,0:T(8,128)(2,1)}), bf16[8,96,576]{2,1,0:T(8,128)(2,1)S(1)}, u32[]{:S(2)}, u32[]{:S(2)}) async-start(bf16[8,96,576]{2,1,0:T(8,128)(2,1)} %bitcast.22), calls=%async_computation.4 | async-start | bytes 1966080 | tf_op jit(solution)/shard_map/all_to_all | solution.py:23
  583.7 47.9 %copy-start.34 = (f32[768]{0:T(1024)S(1)}, f32[768]{0:T(1024)}, u32[]{:S(2)}) copy-start(f32[768]{0:T(1024)} %get-tuple-element.327) | copy-start | bytes 9220
  583.7 71.7 %copy-start.6 = (f32[512,768]{1,0:T(8,128)S(1)}, f32[512,768]{1,0:T(8,128)}, u32[]{:S(2)}) copy-start(f32[512,768]{1,0:T(8,128)} %copy-done.5) | copy-start | bytes 4718596
  (4 other events, 3.2 us)
Sparse Core Ops, SparseCore 0:
  10.4 31.2 all-gather.6
  189.2 38.9 reduce-scatter.4
  356.3 28.5 all-gather.14
  447.4 28.5 all-gather.16
  521.6 37.9 reduce-scatter.10
Sparse Core Ops, SparseCore 1:
  191.8 42.4 all-gather.10
  236.3 26.8 all-gather.8
  265.5 41.5 all-gather.12
  313.7 36.3 reduce-scatter.6
  401.8 37.8 reduce-scatter.8
where the time goes:
time: 676 us; the launch traced here: 666 us
  waiting for transfers between devices  239 us (35%)
  blocking collectives  196 us (29%)
  matrix products  116 us (17%)
  local copies, waits for them, and re-layouts  40.1 us (6%)
  other arithmetic  38.3 us (6%)
  starting transfers between devices  19.6 us (3%)
  between operations  16.4 us (2%)
    psum x1, blocking collectives, shards(): lax.psum((totals[9], totals[10], totals[11], totals[12], totals[13], tota...  41.7 us
    reduce_scatter x1, waiting for transfers between devices, micro_step(): lax.psum_scatter(jnp.dot(context, output_full, preferred_element_type=jnp...  38 us
    reduce_scatter x1, waiting for transfers between devices, micro_step(): lax.psum_scatter(times_trans(pre_grad, up_full).astype(jnp.bfloat16), 'tp...  37.9 us
    reduce_scatter x1, waiting for transfers between devices, micro_step(): lax.psum_scatter(jnp.dot(active, down_full, preferred_element_type=jnp.fl...  36.4 us
    all_gather x1, blocking collectives, shards(): lax.all_gather(value_weight, 'fsdp', axis=0, tiled=True)  35.3 us
    all_gather x1, blocking collectives, shards(): lax.all_gather(query_weight, 'fsdp', axis=0, tiled=True)  33.5 us
    all_gather x1, blocking collectives, shards(): lax.all_gather(output_weight, 'fsdp', axis=1, tiled=True)  33 us
    all_gather x1, blocking collectives, shards(): lax.all_gather(key_weight, 'fsdp', axis=0, tiled=True)  31.4 us
  transfers between devices with their start and end apart: 14, of which 9 were waited for; matrix products, arithmetic and copies ran while one was open for 16% of the time, Pallas kernels for 0%

commit v1 on v0

v1 whole, which is shorter than its diff:
```python
from functools import partial
import math

import jax
import jax.numpy as jnp
import numpy as np
from jax import lax
from jax.experimental import pallas as pl
from jax.experimental.pallas import tpu as pltpu
from jax.sharding import PartitionSpec as P

HD = 64
SEQ = 512
AXES = ("fsdp", "tp")
F32 = jnp.float32
BF16 = jnp.bfloat16
CUTS = 8
MIB = 1 << 20


def exchange_plan(fsdp, tp):
    count = fsdp * tp
    if (fsdp, tp) == (8, 4):
        select, pairs = 1, [(8, 16), (4, 2), (16, 8), (2, 4)]
    else:
        select = tp
        pairs = [(1 << i,) * 2 for i in range(count.bit_length() - 1) if 1 << i != select]
    steps = [[d ^ pair[1 if d & select else 0] for d in range(count)] for pair in pairs]
    steps.append([d ^ select for d in range(count)])
    sources = [[d] for d in range(count)]
    for step in steps:
        sources = [sources[d] + sources[step[d]] for d in range(count)]
    return steps, np.array(sources)


def swap(array, step):
    return lax.ppermute(array, AXES, list(enumerate(step)))


def after(array, *others):
    return lax.optimization_barrier((array, *others))[0]


class Gather:
    def __init__(self, shard, steps):
        self.steps, self.at, self.held, self.pieces = steps, 0, shard[None], None

    def step(self, *others):
        step = self.steps[self.at]
        self.at += 1
        if others:
            self.held = after(self.held, *others)
        moved = swap(self.held, step)
        if self.at == len(self.steps) - 1:
            self.pieces = [self.held, moved]
        else:
            self.held = jnp.concatenate([self.held, moved], axis=0)
        return moved

    def split(self):
        parts = []
        for i in range(self.held.shape[1]):
            part = Gather(self.held[0, i], self.steps)
            part.at, part.held = self.at, self.held[:, i]
            parts.append(part)
        return parts

    def finish(self, *others):
        pieces = [after(piece, *others) for piece in self.pieces] if others else self.pieces
        return self.pieces + [swap(piece, self.steps[-1]) for piece in pieces]


class Sum:
    def __init__(self, keep, send, steps, extra=0):
        self.steps, self.at, self.keep, self.send, self.extra = steps, len(steps) - 1, keep, send, extra

    def add(self, part):
        keep, moved = self.keep[part].astype(F32), self.moved[part].astype(F32)
        if not self.extra:
            return keep + moved
        rows = keep.shape[1] - 2 * self.extra
        total = (keep + moved)[:, :rows]
        high = slice(rows, rows + self.extra)
        low = slice(rows + self.extra, None)
        side = (keep[:, high] + keep[:, low]) + (moved[:, high] + moved[:, low])
        if self.at == 0:
            return total, side
        high = lax.reduce_precision(side, 8, 7)
        return jnp.concatenate([total, high, side - high], axis=1)

    def start(self, *others):
        send = after(self.send, *others) if others else self.send
        self.moved = swap(send, self.steps[self.at])

    def end(self):
        if self.at == 0:
            return self.add(slice(None))
        half = self.keep.shape[0] // 2
        send = self.add(slice(half, None)).astype(BF16)
        keep = self.add(slice(0, half)).astype(BF16)
        self.keep, self.send = keep, send
        self.at -= 1
        return send

    def step(self, *others):
        self.start(*others)
        return self.end()

    @staticmethod
    def merge(*packages):
        one = packages[0]
        keep, send = (
            jnp.stack([getattr(package, name) for package in packages], axis=1) for name in ("keep", "send")
        )
        merged = Sum(keep, send, one.steps)
        merged.at = one.at
        return merged


def both(*packages):
    moved = lax.optimization_barrier([package.moved for package in packages])
    for package, arrived in zip(packages, moved):
        package.moved = arrived
        package.end()


def copy_block(order_ref, from_ref, to_ref):
    to_ref[...] = from_ref[...]


def laid_out(blocks, slot_of, fsdp, tp):
    _, rows, cols = blocks.shape
    grid_spec = pltpu.PrefetchScalarGridSpec(
        num_scalar_prefetch=1,
        grid=(fsdp, tp),
        in_specs=[pl.BlockSpec((1, rows, cols), lambda f, t, s: (s[f * tp + t], 0, 0))],
        out_specs=pl.BlockSpec((1, rows, cols), lambda f, t, s: (f, 0, t)),
    )
    return pl.pallas_call(
        copy_block,
        grid_spec=grid_spec,
        out_shape=jax.ShapeDtypeStruct((fsdp, rows, tp * cols), blocks.dtype),
    )(slot_of, blocks)


def cut_up(full, slot_of, fsdp, tp):
    _, rows, cols = full.shape
    cols = cols // tp
    grid_spec = pltpu.PrefetchScalarGridSpec(
        num_scalar_prefetch=1,
        grid=(fsdp, tp),
        in_specs=[pl.BlockSpec((1, rows, cols), lambda f, t, s: (f, 0, t))],
        out_specs=pl.BlockSpec((1, rows, cols), lambda f, t, s: (s[f * tp + t], 0, 0)),
    )
    return pl.pallas_call(
        copy_block,
        grid_spec=grid_spec,
        out_shape=jax.ShapeDtypeStruct((fsdp * tp, rows, cols), full.dtype),
    )(slot_of, full)


def dot(a, b):
    return lax.dot_general(a, b, (((1,), (0,)), ((), ())), preferred_element_type=F32)


def dot_nt(a, b):
    return lax.dot_general(a, b, (((1,), (1,)), ((), ())), preferred_element_type=F32)


def dot_tn(a, b):
    return lax.dot_general(a, b, (((0,), (0,)), ((), ())), preferred_element_type=F32)


def norm_forward(values):
    average = jnp.mean(values, axis=-1, keepdims=True)
    centered = values - average
    inverse = lax.rsqrt(jnp.mean(centered * centered, axis=-1, keepdims=True) + 1e-12)
    return centered * inverse, inverse


def norm_backward(upstream, normal, inverse, gain):
    scaled = upstream * gain
    return inverse * (
        scaled
        - jnp.mean(scaled, axis=-1, keepdims=True)
        - normal * jnp.mean(scaled * normal, axis=-1, keepdims=True)
    )


def gelu_parts(x):
    below = 0.5 + 0.5 * lax.erf(x * math.sqrt(0.5))
    return x * below, below + x * (jnp.exp(-0.5 * (x * x)) * (1.0 / math.sqrt(2.0 * math.pi)))


def column_sum(array):
    return jnp.sum(array, axis=0, keepdims=True)


def assemble(order_ref, pieces, weight):
    tp = weight.shape[0]
    rows = weight.shape[1] // CUTS
    per = pieces[0].shape[0]
    for i in range(per * len(pieces)):
        block = order_ref[i]
        cut = block // tp
        t = block - cut * tp
        weight[t, pl.ds(pl.multiple_of(cut * rows, rows), rows), :] = pieces[i // per][i % per]


def put_blocks(slot_ref, out_ref, tp, t, value, cols=slice(None)):
    half = out_ref.shape[0]
    rows = value.shape[0] // CUTS
    for cut in range(CUTS):
        slot = lax.rem(slot_ref[cut * tp + t], half)
        out_ref[slot, :rows, cols] = value[cut * rows : (cut + 1) * rows].astype(out_ref.dtype)


def both_halves(turn_ref, keep_ref, send_ref, tp, step):
    for half, out_ref in enumerate((keep_ref, send_ref)):
        lax.fori_loop(
            half * (tp // 2),
            (half + 1) * (tp // 2),
            lambda turn, carry, out_ref=out_ref: (step(turn_ref[turn], out_ref), carry)[1],
            0,
        )


def attention_kernel(
    pieces_n, order_ref, tokens_ref, ids_row, ids_col, bias_ref, output_bias, gain, shift, *rest,
):
    pieces, rest = rest[:pieces_n], rest[pieces_n:]
    (weight, qkv_ref, context_ref, exponent_ref, total_ref, normal_ref, inverse_ref, low_ref, turned_ref, mask,
     acc) = rest
    tp = weight.shape[0]
    cols = context_ref.shape[1]
    assemble(order_ref, pieces, weight)
    mask[...] = jnp.where(ids_col[...] == ids_row[...], 0.0, -1e30)
    acc[...] = tokens_ref[...].astype(F32) + output_bias[...]
    turned_ref[...] = tokens_ref[...].T

    def step(t, carry):
        qkv = (dot(tokens_ref[...], weight[t, :, : 3 * cols]) + bias_ref[t]).astype(BF16)
        qkv_ref[t] = qkv
        contexts = []
        for h in range(cols // HD):
            queries, keys, values = (
                qkv[:, i * cols + h * HD : i * cols + (h + 1) * HD] for i in range(3)
            )
            scores = dot_nt(keys, queries * (HD**-0.5)) + mask[...]
            top = jnp.max(scores, axis=0, keepdims=True)
            exponent = jnp.exp(scores - top)
            total = 1.0 / jnp.sum(exponent, axis=0, keepdims=True)
            exponent = exponent.astype(BF16)
            exponent_ref[t, h] = exponent
            contexts.append((dot_tn(values, exponent) * total).astype(BF16))
            total_ref[t, h : h + 1] = total
        context = jnp.concatenate(contexts, axis=0)
        context_ref[t] = context
        acc[...] += dot_nt(context.T, weight[t, :, 3 * cols :])
        return carry

    lax.fori_loop(0, tp, step, 0)
    normal, inverse = norm_forward(acc[...])
    normal_ref[...] = normal
    inverse_ref[...] = inverse
    low_ref[...] = (normal * gain[...] + shift[...]).astype(BF16)


def up_kernel(pieces_n, order_ref, low_ref, bias_ref, *rest):
    pieces, rest = rest[:pieces_n], rest[pieces_n:]
    weight, active_ref, slope_ref = rest
    tp = weight.shape[0]
    assemble(order_ref, pieces, weight)

    def step(t, carry):
        active, slope = gelu_parts(dot(low_ref[...], weight[t]) + bias_ref[t])
        active_ref[t] = active.astype(BF16)
        slope_ref[t] = slope.astype(BF16)
        return carry

    lax.fori_loop(0, tp, step, 0)


def down_kernel(
    pieces_n, order_ref, slot_ref, turn_ref, active_ref, normal_ref, first_gain, first_shift, bias_ref, gain, shift,
    cotangent_ref, *rest,
):
    pieces, rest = rest[:pieces_n], rest[pieces_n:]
    weight, output_ref, grad_ref, low_ref, sums_ref, keep_ref, send_ref, acc, turned = rest
    tp = weight.shape[0]
    assemble(order_ref, pieces, weight)
    acc[...] = normal_ref[...] * first_gain[...] + (first_shift[...] + bias_ref[...])

    def step(t, carry):
        acc[...] += dot_nt(active_ref[t], weight[t])
        return carry

    lax.fori_loop(0, tp, step, 0)
    normal, inverse = norm_forward(acc[...])
    output_ref[...] = normal * gain[...] + shift[...]
    upstream = cotangent_ref[...].astype(F32)
    grad = norm_backward(upstream, normal, inverse, gain[...])
    grad_ref[...] = grad
    low = grad.astype(BF16)
    low_ref[...] = low
    turned[...] = low.T
    sums_ref[0:1] = column_sum(grad)
    sums_ref[1:2] = column_sum(upstream * normal)
    sums_ref[2:3] = column_sum(upstream)

    def back(t, out_ref):
        put_blocks(slot_ref, out_ref, tp, t, dot(turned[...], active_ref[t]))

    both_halves(turn_ref, keep_ref, send_ref, tp, back)


def middle_kernel(
    slot_ref, turn_ref, grad_ref, low_grad_ref, low_ref, slope_ref, normal_ref, inverse_ref, gain, up_w, down_w,
    resid_ref, resid_low_ref, resid_turned_ref, sums_ref, keep_ref, send_ref, acc, turned,
):
    tp = up_w.shape[0]
    acc[...] = grad_ref[...]
    turned[...] = low_ref[...].T

    def step(t, out_ref):
        wide = dot(low_grad_ref[...], down_w[t]) * slope_ref[t].astype(F32)
        pre_grad = wide.astype(BF16)
        sums_ref[pl.ds(3 + t, 1)] = column_sum(wide)
        put_blocks(slot_ref, out_ref, tp, t, dot(turned[...], pre_grad))
        acc[...] += dot_nt(pre_grad, up_w[t])

    both_halves(turn_ref, keep_ref, send_ref, tp, step)
    grad_one = acc[...]
    normal = normal_ref[...]
    resid = norm_backward(grad_one, normal, inverse_ref[...], gain[...])
    resid_ref[...] = resid
    low = resid.astype(BF16)
    resid_low_ref[...] = low
    resid_turned_ref[...] = low.T
    sums_ref[0:1] = column_sum(resid)
    sums_ref[1:2] = column_sum(grad_one * normal)
    sums_ref[2:3] = column_sum(grad_one)


def attention_back_kernel(
    slot_ref, turn_ref, turned_ref, qkv_ref, context_ref, exponent_ref, total_ref, resid_ref, resid_low_ref,
    resid_turned_ref, sums_in_ref, weight, grad_ref, sums_ref, keep_ref, send_ref,
):
    tp = weight.shape[0]
    cols = context_ref.shape[1]
    grad_ref[...] = resid_ref[...]
    factor = HD**-0.5
    extra = sums_ref.shape[1]
    main = keep_ref.shape[1] - 2 * extra
    half = keep_ref.shape[0]

    def step(t, out_ref):
        outer = dot(resid_low_ref[...], weight[t, :, 3 * cols :])
        totals = total_ref[t].T
        query_grads, key_grads, value_grads = [], [], []
        for h in range(cols // HD):
            at = slice(h * HD, (h + 1) * HD)
            queries, keys, values = (
                qkv_ref[t, :, i * cols + h * HD : i * cols + (h + 1) * HD] for i in range(3)
            )
            queries = queries * factor
            upstream = (outer[:, at] * totals[:, h : h + 1]).astype(BF16)
            row_term = jnp.sum(
                upstream.T.astype(F32) * context_ref[t, at].astype(F32), axis=0, keepdims=True
            )
            exponent = exponent_ref[t, h]
            prob_grad = dot_nt(values, upstream)
            score_grad = (exponent.astype(F32) * (prob_grad - row_term)).astype(BF16)
            key_grads.append(dot(score_grad, queries).astype(BF16))
            value_grads.append(dot(exponent, upstream).astype(BF16))
            query_grads.append((dot_tn(keys, score_grad) * factor).astype(BF16))
        queries = jnp.concatenate(query_grads, axis=0).T
        grad = jnp.concatenate([queries, *key_grads, *value_grads], axis=1)
        grad_ref[...] += dot_nt(grad, weight[t, :, : 3 * cols])
        put_blocks(slot_ref, out_ref, tp, t, dot(turned_ref[...], grad), slice(0, 3 * cols))
        out_grad = dot_nt(resid_turned_ref[...], context_ref[t])
        put_blocks(slot_ref, out_ref, tp, t, out_grad, slice(3 * cols, None))
        columns = column_sum(grad.astype(F32))
        side = jnp.concatenate([columns, jnp.zeros((1, cols), F32)], axis=1)
        side = jnp.concatenate([sums_in_ref[t], side], axis=0)
        sums_ref[t] = side
        high = side.astype(BF16)
        low = (side - high.astype(F32)).astype(BF16)
        side = jnp.concatenate([high, low], axis=0)
        for cut in range(CUTS):
            out_ref[lax.rem(slot_ref[cut * tp + t], half), main:, :] = side

    both_halves(turn_ref, keep_ref, send_ref, tp, step)


def call(kernel, pieces, scalars, inputs, outs, scratch, flops, limit=22):
    whole = pl.BlockSpec(memory_space=pltpu.VMEM)
    smem = pl.BlockSpec(memory_space=pltpu.SMEM)
    return pl.pallas_call(
        kernel,
        in_specs=[smem] * len(scalars) + [whole] * len(inputs) + [whole] * len(pieces),
        out_specs=[whole] * len(outs),
        out_shape=[jax.ShapeDtypeStruct(*out) for out in outs],
        scratch_shapes=scratch,
        compiler_params=pltpu.CompilerParams(vmem_limit_bytes=limit * MIB),
        cost_estimate=pl.CostEstimate(flops=flops, bytes_accessed=16 * MIB, transcendentals=0),
    )(*scalars, *inputs, *pieces)


def shards(
    steps,
    sources,
    fsdp,
    tp,
    tokens,
    segment_ids,
    query_weight,
    key_weight,
    value_weight,
    query_bias,
    value_bias,
    output_weight,
    output_bias,
    first_gain,
    first_shift,
    up_weight,
    up_bias,
    down_weight,
    down_bias,
    second_gain,
    second_shift,
    cotangent,
):
    rows, cols = query_weight.shape
    width = rows * fsdp
    units = up_weight.shape[1]
    count = fsdp * tp
    cut_rows = width // CUTS
    blocks_n = CUTS * tp
    direct = blocks_n == count
    place = lax.axis_index("tp")
    me = lax.axis_index("fsdp") * tp + place
    doc_ids = lax.dynamic_slice_in_dim(segment_ids, place * SEQ, SEQ)

    def mine(table):
        return lax.dynamic_index_in_dim(jnp.asarray(table, jnp.int32), me, keepdims=False)

    slot_of = mine(np.argsort(sources, axis=1))
    if direct:
        order, slots = mine(sources), slot_of
        turns = mine(np.argsort(np.argsort(sources, axis=1)[:, :tp] // (count // 2), axis=1, kind="stable"))
    else:
        cut, t = np.divmod(np.arange(blocks_n), tp)
        kept = tp // 2
        order = jnp.arange(blocks_n, dtype=jnp.int32)
        slots = jnp.asarray(t // kept * (CUTS * kept) + cut * kept + t % kept, jnp.int32)
        turns = jnp.arange(tp, dtype=jnp.int32)

    def ready(pieces):
        if direct:
            return pieces
        full = laid_out(jnp.concatenate(pieces, axis=0), slot_of, fsdp, tp)
        full = full.reshape(CUTS, cut_rows, tp, -1).transpose(0, 2, 1, 3)
        return [full.reshape(blocks_n, cut_rows, -1)]

    def outgoing(keep, send, extra=0):
        if direct:
            return Sum(keep, send, steps, extra)
        blocks = jnp.concatenate([keep, send], axis=0)[:, :cut_rows]
        full = blocks.reshape(2, CUTS, tp // 2, cut_rows, -1).transpose(1, 3, 0, 2, 4)
        blocks = cut_up(full.reshape(fsdp, rows, -1), slot_of, fsdp, tp)
        return Sum(blocks[: count // 2], blocks[count // 2 :], steps)

    query_bias, value_bias = query_bias.reshape(tp, 1, cols), value_bias.reshape(tp, 1, cols)
    blank = jnp.zeros_like(query_bias)
    qkv_bias = jnp.concatenate([query_bias, blank, value_bias], axis=2)
    up_bias = up_bias.reshape(tp, 1, units)
    vectors = jnp.stack(
        [output_bias, first_gain, first_shift, down_bias, second_gain, second_shift]
    ).reshape(6, 1, width)
    output_bias, first_gain, first_shift, down_bias, second_gain, second_shift = (
        vectors[i] for i in range(6)
    )
    ids_row, ids_col = doc_ids.reshape(1, -1), doc_ids.reshape(-1, 1)

    a = Gather(jnp.concatenate([query_weight, key_weight, value_weight, output_weight.T], axis=1), steps)
    b = Gather(up_weight, steps)
    c = Gather(down_weight.T, steps)
    if direct:
        pair = Gather(jnp.stack([up_weight, down_weight.T]), steps)
        first = a.step()
        pair.held = after(pair.held, first)
        a_x = a.step(qkv_bias, up_bias, vectors, ids_row, ids_col)
        pair.step()
        a.held, pair.held = lax.optimization_barrier((a.held, pair.held))
        a.step()
        pair.step()
        a.held, pair.held = lax.optimization_barrier((a.held, pair.held))
        b, c = pair.split()
        a_x = a.step()
        b_z = b.step()
        a.pieces, b.held = lax.optimization_barrier((a.pieces, b.held))
        attn_w = ready(a.finish())
        b_x = b.step()
        c_z = c.step(b_z)
    else:
        for package in (a, b, c):
            for _ in steps[:-1]:
                package.step()
        attn_w = ready(a.finish())
    pieces_n = len(attn_w)

    weight = ((tp, width, units), BF16)
    state = pltpu.VMEM((SEQ, width), F32)
    turned = pltpu.VMEM((width, SEQ), BF16)
    mask = pltpu.VMEM((SEQ, SEQ), F32)
    wide = (SEQ, width)
    flops = 2 * SEQ * width * width
    attn_full, qkv, context, exponent, total, normal, inverse, low, tokens_turned = call(
        partial(attention_kernel, pieces_n),
        attn_w,
        (order,),
        (tokens, ids_row, ids_col, qkv_bias, output_bias, first_gain, first_shift),
        [weight, ((tp, SEQ, 3 * cols), BF16), ((tp, cols, SEQ), BF16),
         ((tp, cols // HD, SEQ, SEQ), BF16), ((tp, 8, SEQ), F32), (wide, F32),
         ((SEQ, 1), F32), (wide, BF16), ((width, SEQ), BF16)],
        [mask, state],
        8 * flops,
    )
    if direct:
        up_w = b.finish(inverse)
        c.step(inverse, b_x)
    else:
        up_w = ready(b.finish())
    up_full, active, slope = call(
        partial(up_kernel, pieces_n),
        up_w,
        (order,),
        (low, up_bias),
        [weight, ((tp, SEQ, units), BF16), ((tp, SEQ, units), BF16)],
        [],
        5 * flops,
    )
    down_w = c.finish(slope) if direct else ready(c.finish())
    half = ((blocks_n // 2, cut_rows, units), BF16)
    down_full, layer_output, grad_two, grad_low, down_sums, *down_blocks = call(
        partial(down_kernel, pieces_n),
        down_w,
        (order, slots, turns),
        (active, normal, first_gain, first_shift, down_bias, second_gain, second_shift, cotangent),
        [weight, (wide, F32), (wide, F32), (wide, BF16), ((8, width), F32), half, half],
        [state, turned],
        10 * flops,
    )
    down_sum = outgoing(*down_blocks)
    if direct:
        first = down_sum.step()
        down_sum.start()
        grad_low = after(grad_low, first)
    resid, resid_low, resid_turned, middle_sums, *up_blocks = call(
        middle_kernel,
        [up_full, down_full],
        (slots, turns),
        (grad_two, grad_low, low, slope, normal, inverse, first_gain),
        [(wide, F32), (wide, BF16), ((width, SEQ), BF16), ((8, width), F32), half, half],
        [state, turned],
        12 * flops,
    )
    up_sum = outgoing(*up_blocks)
    if direct:
        moved = down_sum.moved
        sent = down_sum.end()
        down_sum.start(middle_sums)
        first = up_sum.step(moved)
        up_sum.start()
        resid_low = after(resid_low, first, sent)
    sides = jnp.broadcast_to(jnp.concatenate([down_sums[:3], middle_sums[:3]], axis=0), (tp, 6, width))
    sides = jnp.concatenate([sides, middle_sums[3 : 3 + tp, None]], axis=1)
    part = ((blocks_n // 2, cut_rows + 16, units), BF16)
    input_grad, side, *attn_blocks = call(
        attention_back_kernel,
        [attn_full],
        (slots, turns),
        (tokens_turned, qkv, context, exponent, total, resid, resid_low, resid_turned, sides),
        [(wide, F32), ((tp, 8, units), F32), part, part],
        [],
        20 * flops,
    )
    attn_sum = outgoing(*attn_blocks, 8)
    if direct:
        attn_sum.step(down_sum.moved, up_sum.moved)
        down_sum.end()
        up_sum.end()
        attn_sum.start()
        up_sum.start()
        both(attn_sum, up_sum)
        pair = Sum.merge(down_sum, up_sum)
        attn_sum.start()
        pair.start()
        both(attn_sum, pair)
        attn_sum.start()
        pair.start()
        attn_sum.end()
        finals = [[part] for part in pair.end()[0]]
        attn_sum.start()
        finals.append(attn_sum.end())
    else:
        finals = []
        for package in (down_sum, up_sum, attn_sum):
            while package.at > 0:
                package.step()
            package.start()
            finals.append(package.end())
    if direct:
        attn_grad, side = finals[2][0][0], finals[2][1][0]
    else:
        attn_grad = finals[2][0]
        side = lax.dynamic_index_in_dim(lax.psum(side, AXES), place, keepdims=False)
    return (
        layer_output,
        input_grad,
        attn_grad[:, :cols],
        attn_grad[:, cols : 2 * cols],
        attn_grad[:, 2 * cols : 3 * cols],
        side[7, :cols],
        side[7, 2 * cols : 3 * cols],
        attn_grad[:, 3 * cols :].T,
        side[3],
        side[4],
        side[5],
        finals[1][0],
        side[6],
        finals[0][0].T,
        side[0],
        side[1],
        side[2],
    )


def solution(mesh):
    fsdp, tp = mesh.shape["fsdp"], mesh.shape["tp"]
    steps, sources = exchange_plan(fsdp, tp)
    both, up, down = P(AXES, None), P("fsdp", "tp"), P("tp", "fsdp")
    return jax.shard_map(
        partial(shards, steps, sources, fsdp, tp),
        mesh=mesh,
        in_specs=(
            both, P("fsdp"), up, up, up, P(), P(), down, P(), P(), P(), up, P(), down, P(), P(), P(), both,
        ),
        out_specs=(
            both, both, up, up, up, P("tp"), P("tp"), down, P(), P(), P(), up, P("tp"), down, P(), P(), P(),
        ),
        check_vma=False,
    )
```

time: 676 us -> 232 us (0.34); the launches traced: 666 us -> 230 us
  blocking collectives: 196 us -> 0 us
  waiting for transfers between devices: 239 us -> 114 us
  matrix products: 116 us -> 0 us
  Pallas kernels: 0 us -> 59.6 us
  other arithmetic: 38.3 us -> 9.9 us
  local copies, waits for them, and re-layouts: 40.1 us -> 17.4 us
  between operations: 16.4 us -> 1.33 us
  starting transfers between devices: 19.6 us -> 27.8 us
    all_gather x4 -> x0, blocking collectives: 133 us -> none  [the longest x1 35.3 us: shards(): lax.all_gather(value_weight, 'fsdp', axis=0, tiled=True)]
    dot_general x46 -> x0, matrix products: 116 us -> none  [the longest x6 23.1 us: times_trans(): lax.dot_general(former, latter, (((1,), (1,)), ((), ())), preferred_eleme...]
    ppermute x0 -> x29, waiting for transfers between devices: none -> 114 us  [swap(): return lax.ppermute(array, AXES, list(enumerate(step)))]
    reduce_scatter x4 -> x0, waiting for transfers between devices: 112 us -> none  [the longest x1 38 us: micro_step(): lax.psum_scatter(jnp.dot(context, output_full, preferred_element_type=jnp...]
    all_gather x6 -> x0, waiting for transfers between devices: 97.2 us -> none  [the longest x1 28.5 us: micro_step(): grad_rows = lax.all_gather(grad_low, 'tp', axis=0, tiled=True)]
    psum x2 -> x0, blocking collectives: 62.9 us -> none  [the longest x1 41.7 us: shards(): lax.psum((totals[9], totals[10], totals[11], totals[12], totals[13], tota...]
    pallas_call x0 -> x5, Pallas kernels: none -> 59.6 us  [call(): pl.pallas_call(kernel, in_specs=[smem] * len(scalars) + [whole] * len(inp...]
    ppermute x0 -> x29, starting transfers between devices: none -> 27.8 us  [swap(): return lax.ppermute(array, AXES, list(enumerate(step)))]
  transfers between devices with their start and end apart: 14 -> 29, of which waited for: 9 -> 20; matrix products, arithmetic and copies ran while one was open for 16% -> 4% of each run, Pallas kernels for 0% -> 22%
where the time goes in v1:
time: 232 us; the launch traced here: 230 us
  waiting for transfers between devices  114 us (49%)
  Pallas kernels  59.6 us (26%)
  starting transfers between devices  27.8 us (12%)
  local copies, waits for them, and re-layouts  17.4 us (7%)
  other arithmetic  9.9 us (4%)
    ppermute x29, waiting for transfers between devices, swap(): return lax.ppermute(array, AXES, list(enumerate(step)))  114 us
    pallas_call x5, Pallas kernels, call(): pl.pallas_call(kernel, in_specs=[smem] * len(scalars) + [whole] * len(inp...  59.6 us
    ppermute x29, starting transfers between devices, swap(): return lax.ppermute(array, AXES, list(enumerate(step)))  27.8 us
    unnamed x44, local copies, waits for them, and re-layouts  9.01 us
  transfers between devices with their start and end apart: 29, of which 20 were waited for; matrix products, arithmetic and copies ran while one was open for 4% of the time, Pallas kernels for 22%

profile of v1, /device:TPU:0, one launch (start us, length us, event | category | flops | bytes accessed | tf_op | source)
XLA Modules:
  0.0 230.4 jit_solution(14367942737922782314)
XLA Ops:
  0.7 0.9 copy.40
  1.5 1.0 maximum_bitcast_fusion.1
  2.5 3.1 %collective-permute-start = (bf16[1,96,768]{2,1,0:T(8,128)(2,1)S(1)}, bf16[1,96,768]{2,1,0:T(8,128)(2,1)S(1)}, u32[]{:S(2)}, u32[]{:S(2)}) collective-permute-start(bf16[1,96,768]{2,1,0:T(8,128)(2,1)S(1)} %maximum_bitcast_fusion.1), channel_id=1, source_target_pairs={{0,8},{1,17},{2,10},{3,19},{4,12},{5,21},{6,14},{7,23},{8,0},{9,25... | collective-permute-start | bytes 442376 | tf_op jit(solution)/shard_map/ppermute | solution.py:37
  7.2 1.0 maximum_bitcast_fusion
  8.2 1.7 collective-permute-done
  9.9 2.3 collective-permute-start.2
  13.0 1.6 collective-permute-start.1
  14.6 5.4 %collective-permute-done.2 = bf16[1,2,96,768]{3,2,0,1:T(8,128)(2,1)S(1)} collective-permute-done((bf16[1,2,96,768]{3,2,0,1:T(8,128)(2,1)S(1)}, bf16[1,2,96,768]{3,2,0,1:T(8,128)(2,1)S(1)}, u32[]{:S(2)}, u32[]{:S(2)}) %collective-permute-start.2) | collective-permute-done | bytes 294944 | tf_op jit(solution)/shard_map/ppermute | solution.py:37
  20.1 2.4 %collective-permute-start.3 = (bf16[4,96,768]{2,1,0:T(8,128)(2,1)S(1)}, bf16[4,96,768]{2,1,0:T(8,128)(2,1)S(1)}, u32[]{:S(2)}, u32[]{:S(2)}) collective-permute-start(bf16[4,96,768]{2,1,0:T(8,128)(2,1)S(1)} %pad_maximum_fusion.8), channel_id=1, source_target_pairs={{0,16},{1,9},{2,18},{3,11},{4,20},{5,13},{6,22},{7,15},{8,24},{9,1... | collective-permute-start | bytes 1769480 | tf_op jit(solution)/shard_map/ppermute | solution.py:37
  22.5 1.5 collective-permute-start.4
  24.0 13.3 %collective-permute-done.3 = bf16[4,96,768]{2,1,0:T(8,128)(2,1)S(1)} collective-permute-done((bf16[4,96,768]{2,1,0:T(8,128)(2,1)S(1)}, bf16[4,96,768]{2,1,0:T(8,128)(2,1)S(1)}, u32[]{:S(2)}, u32[]{:S(2)}) %collective-permute-start.3) | collective-permute-done | bytes 589856 | tf_op jit(solution)/shard_map/ppermute | solution.py:37
  37.5 1.8 collective-permute-start.5
  39.3 0.9 slice_bitcast_fusion
  40.3 17.1 %collective-permute-done.6 = bf16[4,96,768]{2,1,0:T(8,128)(2,1)S(1)} collective-permute-done((bf16[4,96,768]{2,1,0:T(8,128)(2,1)S(1)}, bf16[4,96,768]{2,1,0:T(8,128)(2,1)S(1)}, u32[]{:S(2)}, u32[]{:S(2)}) %collective-permute-start.6) | collective-permute-done | bytes 589856 | tf_op jit(solution)/shard_map/ppermute | solution.py:37
  59.3 2.1 collective-permute-done.7.rest_2_
  61.4 1.0 collective-permute-done.8.rest_3_
  62.4 14.2 %shard_map.332 = (bf16[4,768,768]{2,1,0:T(8,128)(2,1)S(1)}, bf16[4,512,576]{2,1,0:T(8,128)(2,1)S(1)}, bf16[4,192,512]{2,1,0:T(8,128)(2,1)S(1)}, bf16[4,3,512,512...) custom-call(s32[32]{0:T(128)S(1)} %fusion.31.order_ref, ...), custom_call_target="tpu_custom_call" | custom-call | flops 4831838208 | bytes 16777216 | tf_op jit(solution)/shard_map/pallas_call | solution.py:399
  76.7 2.2 copy-done.3
  78.8 0.9 copy-done.11
  80.8 2.2 collective-permute-done.10.rest_2_
  83.0 1.6 collective-permute-done.11.rest_3_
  84.6 6.4 %shard_map.333 = (bf16[4,768,768]{2,1,0:T(8,128)(2,1)S(1)}, bf16[4,512,768]{2,1,0:T(8,128)(2,1)S(1)}, bf16[4,512,768]{2,1,0:T(8,128)(2,1)S(1)}) custom-call(s32[32]{0:T(128)S(1)} %fusion.31.order_ref, bf16[512,768]{1,0:T(8,128)(2,1)S(1)} %get-tuple-element.77.low_ref, f32[4,1,768]{2,1,0:T(1,128)S(1)} %bitcast.45, ...), custom_call_target="tpu_custom_call" | custom-call | flops 3019898880 | bytes 16777216 | tf_op jit(solution)/shard_map/pallas_call | solution.py:399
  91.0 5.6 %collective-permute-done.13.rest_1_ = bf16[8,96,768]{2,1,0:T(8,128)(2,1)S(1)} collective-permute-done((bf16[8,96,768]{2,1,0:T(8,128)(2,1)S(1)}, bf16[8,96,768]{2,1,0:T(8,128)(2,1)S(1)}, u32[]{:S(2)}, u32[]{:S(2)}) %collective-permute-start.13) | collective-permute-done | bytes 1179680 | tf_op jit(solution)/shard_map/ppermute | solution.py:37
  98.6 0.9 collective-permute-done.14.rest_2_
  99.5 1.7 collective-permute-done.15.rest_3_
  101.2 1.4 copy-done.8
  102.6 9.9 %shard_map.334 = (bf16[4,768,768]{2,1,0:T(8,128)(2,1)S(1)}, f32[512,768]{1,0:T(8,128)}, f32[512,768]{1,0:T(8,128)S(1)}, bf16[512,768]{1,0:T(8,128)(2,1)S(1)}, f3...) custom-call(s32[32]{0:T(128)S(1)} %fusion.31.order_ref, ...), custom_call_target="tpu_custom_call" | custom-call | flops 6039797760 | bytes 16777216 | tf_op jit(solution)/shard_map/pallas_call | solution.py:399
  112.6 4.4 %collective-permute-done.16 = bf16[16,96,768]{2,1,0:T(8,128)(2,1)S(1)} collective-permute-done((bf16[16,96,768]{2,1,0:T(8,128)(2,1)S(1)}, bf16[16,96,768]{2,1,0:T(8,128)(2,1)S(1)}, u32[]{:S(2)}, u32[]{:S(2)}) %collective-permute-start.16) | collective-permute-done | bytes 2359328 | tf_op jit(solution)/shard_map/ppermute | solution.py:37
  117.0 1.8 add_convert_fusion.1
  119.1 10.7 %shard_map.335 = (f32[512,768]{1,0:T(8,128)S(1)}, bf16[512,768]{1,0:T(8,128)(2,1)S(1)}, bf16[768,512]{1,0:T(8,128)(2,1)S(1)}, f32[8,768]{1,0:T(8,128)S(1)}, bf16...) custom-call(s32[32]{0:T(128)S(1)} %fusion.32.slot_ref, s32[4]{0:T(128)S(1)} %fusion.33.turn_ref, ...), custom_call_target="tpu_custom_call" | custom-call | flops 7247757312 | bytes 16777216 | tf_op jit(solution)/shard_map/pallas_call | solution.py:399
  129.8 5.2 %collective-permute-done.17 = bf16[8,96,768]{2,1,0:T(8,128)(2,1)S(1)} collective-permute-done((bf16[8,96,768]{2,1,0:T(8,128)(2,1)S(1)}, bf16[8,96,768]{2,1,0:T(8,128)(2,1)S(1)}, u32[]{:S(2)}, u32[]{:S(2)}) %collective-permute-start.17) | collective-permute-done | bytes 1179680 | tf_op jit(solution)/shard_map/ppermute | solution.py:37
  135.1 4.4 %collective-permute-done.18 = bf16[16,96,768]{2,1,0:T(8,128)(2,1)S(1)} collective-permute-done((bf16[16,96,768]{2,1,0:T(8,128)(2,1)S(1)}, bf16[16,96,768]{2,1,0:T(8,128)(2,1)S(1)}, u32[]{:S(2)}, u32[]{:S(2)}) %collective-permute-start.18) | collective-permute-done | bytes 2359328 | tf_op jit(solution)/shard_map/ppermute | solution.py:37
  141.1 1.2 collective-permute-start.19
  142.7 2.3 %copy-done.4 = bf16[4,768,768]{2,1,0:T(8,128)(2,1)S(1)} copy-done((bf16[4,768,768]{2,1,0:T(8,128)(2,1)S(1)}, bf16[4,768,768]{2,1,0:T(8,128)(2,1)}, u32[]{:S(2)}) %copy-start.4) | copy-done | bytes 4718616
  145.1 18.4 %shard_map.336 = (f32[512,768]{1,0:T(8,128)}, f32[4,8,768]{2,1,0:T(8,128)}, bf16[16,112,768]{2,1,0:T(8,128)(2,1)S(1)}, bf16[16,112,768]{2,1,0:T(8,128)(2,1)S(1)}) custom-call(s32[32]{0:T(128)S(1)} %fusion.32.slot_ref, s32[4]{0:T(128)S(1)} %fusion.33.turn_ref, bf16[768,512]{1,0:T(8,128)(2,1)S(1)} %copy-done.12, bf16[4,512,576]{2,1,0:T(8,128)(2,1)S(1)} %copy-done.10, ...), custom_call_target="tpu_custom_call" | custom-call | flops 12079595520 | bytes 16777216 | tf_op jit(solution)/shard_map/pallas_call | solution.py:399
  163.5 1.0 collective-permute-start.21
  164.9 4.3 %collective-permute-done.21 = bf16[16,112,768]{2,1,0:T(8,128)(2,1)S(1)} collective-permute-done((bf16[16,112,768]{2,1,0:T(8,128)(2,1)S(1)}, bf16[16,112,768]{2,1,0:T(8,128)(2,1)S(1)}, u32[]{:S(2)}, u32[]{:S(2)}) %collective-permute-start.21) | collective-permute-done | bytes 2752544 | tf_op jit(solution)/shard_map/ppermute | solution.py:37
  170.2 1.1 collective-permute-start.22
  171.6 1.5 collective-permute-start.23
  173.6 15.1 %collective-permute-done.23 = bf16[4,96,768]{2,1,0:T(8,128)(2,1)S(1)} collective-permute-done((bf16[4,96,768]{2,1,0:T(8,128)(2,1)S(1)}, bf16[4,96,768]{2,1,0:T(8,128)(2,1)S(1)}, u32[]{:S(2)}, u32[]{:S(2)}) %collective-permute-start.23) | collective-permute-done | bytes 589856 | tf_op jit(solution)/shard_map/ppermute | solution.py:37
  191.0 1.5 collective-permute-start.25
  192.7 8.3 %collective-permute-done.25 = bf16[2,2,96,768]{3,2,0,1:T(8,128)(2,1)S(1)} collective-permute-done((bf16[2,2,96,768]{3,2,0,1:T(8,128)(2,1)S(1)}, bf16[2,2,96,768]{3,2,0,1:T(8,128)(2,1)S(1)}, u32[]{:S(2)}, u32[]{:S(2)}) %collective-permute-start.25) | collective-permute-done | bytes 589856 | tf_op jit(solution)/shard_map/ppermute | solution.py:37
  200.9 12.3 %collective-permute-done.24 = bf16[4,112,768]{2,1,0:T(8,128)(2,1)S(1)} collective-permute-done((bf16[4,112,768]{2,1,0:T(8,128)(2,1)S(1)}, bf16[4,112,768]{2,1,0:T(8,128)(2,1)S(1)}, u32[]{:S(2)}, u32[]{:S(2)}) %collective-permute-start.24) | collective-permute-done | bytes 688160 | tf_op jit(solution)/shard_map/ppermute | solution.py:37
  213.8 2.8 %collective-permute-start.26 = (bf16[2,112,768]{2,1,0:T(8,128)(2,1)S(1)}, bf16[2,112,768]{2,1,0:T(8,128)(2,1)S(1)}, u32[]{:S(2)}, u32[]{:S(2)}) collective-permute-start(bf16[2,112,768]{2,1,0:T(8,128)(2,1)S(1)} %pad_maximum_fusion.12), channel_id=1, source_target_pairs={{0,4},{1,3},{2,6},{3,1},{4,0},{5,7},{6,2},{7,5},{8,12},{9,11},{10,... | collective-permute-start | bytes 1032200 | tf_op jit(solution)/shard_map/ppermute | solution.py:37
  216.7 4.3 %collective-permute-done.28 = bf16[1,2,96,768]{3,2,0,1:T(8,128)(2,1)S(1)} collective-permute-done((bf16[1,2,96,768]{3,2,0,1:T(8,128)(2,1)S(1)}, bf16[1,2,96,768]{3,2,0,1:T(8,128)(2,1)S(1)}, u32[]{:S(2)}, u32[]{:S(2)}) %collective-permute-start.28) | collective-permute-done | bytes 294944 | tf_op jit(solution)/shard_map/ppermute | solution.py:37
  221.0 0.8 slice_bitcast_fusion.2
  222.1 2.0 collective-permute-start.27
  224.1 3.4 %collective-permute-done.27 = bf16[1,112,768]{2,1,0:T(8,128)(2,1)S(1)} collective-permute-done((bf16[1,112,768]{2,1,0:T(8,128)(2,1)S(1)}, bf16[1,112,768]{2,1,0:T(8,128)(2,1)S(1)}, u32[]{:S(2)}, u32[]{:S(2)}) %collective-permute-start.27) | collective-permute-done | bytes 172064 | tf_op jit(solution)/shard_map/ppermute | solution.py:37
  (146 shorter events, 18.4 us)
Async XLA Ops:
  2.5 7.4 %collective-permute-start = (bf16[1,96,768]{2,1,0:T(8,128)(2,1)S(1)}, bf16[1,96,768]{2,1,0:T(8,128)(2,1)S(1)}, u32[]{:S(2)}, u32[]{:S(2)}) collective-permute-start(bf16[1,96,768]{2,1,0:T(8,128)(2,1)S(1)} %maximum_bitcast_fusion.1), channel_id=1, source_target_pairs={{0,8},{1,17},{2,10},{3,19},{4,12},{5,21},{6,14},{7,23},{8,0},{9,25... | collective-permute-start | bytes 442376 | tf_op jit(solution)/shard_map/ppermute | solution.py:37
  9.9 10.0 %collective-permute-start.2 = (bf16[1,2,96,768]{3,2,0,1:T(8,128)(2,1)S(1)}, bf16[1,2,96,768]{3,2,0,1:T(8,128)(2,1)S(1)}, u32[]{:S(2)}, u32[]{:S(2)}) collective-permute-start(bf16[1,2,96,768]{3,2,0,1:T(8,128)(2,1)S(1)} %maximum_bitcast_fusion), channel_id=1, source_target_pairs={{0,8},{1,17},{2,10},{3,19},{4,12},{5,21},{6,14},{7,23},{8,0},{9,25... | collective-permute-start | bytes 884744 | tf_op jit(solution)/shard_map/ppermute | solution.py:37
  13.0 7.0 %collective-permute-start.1 = (bf16[2,96,768]{2,1,0:T(8,128)(2,1)S(1)}, bf16[2,96,768]{2,1,0:T(8,128)(2,1)S(1)}, u32[]{:S(2)}, u32[]{:S(2)}) collective-permute-start(bf16[2,96,768]{2,1,0:T(8,128)(2,1)S(1)} %pad_maximum_fusion.14), channel_id=1, source_target_pairs={{0,4},{1,3},{2,6},{3,1},{4,0},{5,7},{6,2},{7,5},{8,12},{9,11},{10,... | collective-permute-start | bytes 884744 | tf_op jit(solution)/shard_map/ppermute | solution.py:37
  20.1 17.2 %collective-permute-start.3 = (bf16[4,96,768]{2,1,0:T(8,128)(2,1)S(1)}, bf16[4,96,768]{2,1,0:T(8,128)(2,1)S(1)}, u32[]{:S(2)}, u32[]{:S(2)}) collective-permute-start(bf16[4,96,768]{2,1,0:T(8,128)(2,1)S(1)} %pad_maximum_fusion.8), channel_id=1, source_target_pairs={{0,16},{1,9},{2,18},{3,11},{4,20},{5,13},{6,22},{7,15},{8,24},{9,1... | collective-permute-start | bytes 1769480 | tf_op jit(solution)/shard_map/ppermute | solution.py:37
  22.5 14.9 %collective-permute-start.4 = (bf16[2,2,96,768]{3,2,0,1:T(8,128)(2,1)S(1)}, bf16[2,2,96,768]{3,2,0,1:T(8,128)(2,1)S(1)}, u32[]{:S(2)}, u32[]{:S(2)}) collective-permute-start(bf16[2,2,96,768]{3,2,0,1:T(8,128)(2,1)S(1)} %pad_maximum_fusion.9), channel_id=1, source_target_pairs={{0,4},{1,3},{2,6},{3,1},{4,0},{5,7},{6,2},{7,5},{8,12},{9,11},{10,... | collective-permute-start | bytes 1769480 | tf_op jit(solution)/shard_map/ppermute | solution.py:37
  37.5 19.9 %collective-permute-start.5 = (bf16[8,96,768]{2,1,0:T(8,128)(2,1)S(1)}, bf16[8,96,768]{2,1,0:T(8,128)(2,1)}, u32[]{:S(2)}, u32[]{:S(2)}) collective-permute-start(bf16[8,96,768]{2,1,0:T(8,128)(2,1)S(1)} %pad_maximum_fusion.2.rest_0_), channel_id=1, source_target_pairs={{0,2},{1,5},{2,0},{3,7},{4,6},{5,1},{6,4},{7,3},{8,10},{9,13},{10,... | collective-permute-start | bytes 3538952 | tf_op jit(solution)/shard_map/ppermute | solution.py:37
  40.2 18.4 %copy-start.15 = (f32[768]{0:T(1024)S(1)}, f32[768]{0:T(1024)}, u32[]{:S(2)}) copy-start(f32[768]{0:T(1024)} %param.30) | copy-start | bytes 9220
  40.2 18.4 %copy-start.16 = (f32[768]{0:T(1024)S(1)}, f32[768]{0:T(1024)}, u32[]{:S(2)}) copy-start(f32[768]{0:T(1024)} %param.31) | copy-start | bytes 9220
  40.2 18.4 %copy-start.17 = (f32[768]{0:T(1024)S(1)}, f32[768]{0:T(1024)}, u32[]{:S(2)}) copy-start(f32[768]{0:T(1024)} %param.29) | copy-start | bytes 9220
  40.2 22.2 %copy-start = (bf16[512,768]{1,0:T(8,128)(2,1)S(1)}, bf16[512,768]{1,0:T(8,128)(2,1)}, u32[]{:S(2)}) copy-start(bf16[512,768]{1,0:T(8,128)(2,1)} %tokens_ref.1) | copy-start | bytes 2359300
  40.2 17.2 %collective-permute-start.6 = (bf16[4,96,768]{2,1,0:T(8,128)(2,1)S(1)}, bf16[4,96,768]{2,1,0:T(8,128)(2,1)S(1)}, u32[]{:S(2)}, u32[]{:S(2)}) collective-permute-start(bf16[4,96,768]{2,1,0:T(8,128)(2,1)S(1)} %get-tuple-element.199), channel_id=1, source_target_pairs={{0,16},{1,9},{2,18},{3,11},{4,20},{5,13},{6,22},{7,15},{8,24},{9,1... | collective-permute-start | bytes 1769480 | tf_op jit(solution)/shard_map/ppermute | solution.py:37
  57.5 3.9 %collective-permute-start.7 = (bf16[8,96,768]{2,1,0:T(8,128)(2,1)S(1)}, bf16[8,96,768]{2,1,0:T(8,128)(2,1)}, u32[]{:S(2)}, u32[]{:S(2)}) collective-permute-start(bf16[8,96,768]{2,1,0:T(8,128)(2,1)S(1)} %pad_maximum_fusion.2.rest_0_), channel_id=1, source_target_pairs={{0,1},{1,0},{2,3},{3,2},{4,5},{5,4},{6,7},{7,6},{8,9},{9,8},{10,11... | collective-permute-start | bytes 3538952 | tf_op jit(solution)/shard_map/ppermute | solution.py:37
  57.6 4.9 %collective-permute-start.8 = (bf16[8,96,768]{2,1,0:T(8,128)(2,1)}, bf16[8,96,768]{2,1,0:T(8,128)(2,1)}, u32[]{:S(2)}, u32[]{:S(2)}) collective-permute-start(bf16[8,96,768]{2,1,0:T(8,128)(2,1)} %collective-permute-done.5.rest_1_), channel_id=1, source_target_pairs={{0,1},{1,0},{2,3},{3,2},{4,5},{5,4},{6,7},{7,6},{8,9},{9,8},{10,11... | collective-permute-start | bytes 3538952 | tf_op jit(solution)/shard_map/ppermute | solution.py:37
  58.1 21.7 %collective-permute-start.9 = (bf16[8,96,768]{2,1,0:T(8,128)(2,1)S(1)}, bf16[8,96,768]{2,1,0:T(8,128)(2,1)}, u32[]{:S(2)}, u32[]{:S(2)}) collective-permute-start(bf16[8,96,768]{2,1,0:T(8,128)(2,1)S(1)} %pad_maximum_fusion.4.rest_0_), channel_id=1, source_target_pairs={{0,2},{1,5},{2,0},{3,7},{4,6},{5,1},{6,4},{7,3},{8,10},{9,13},{10,... | collective-permute-start | bytes 3538952 | tf_op jit(solution)/shard_map/ppermute | solution.py:37
  59.3 21.0 %copy-start.14 = (bf16[4,96,768]{2,1,0:T(8,128)(2,1)S(1)}, bf16[4,96,768]{2,1,0:T(8,128)(2,1)}, u32[]{:S(2)}) copy-start(bf16[4,96,768]{2,1,0:T(8,128)(2,1)} %get-tuple-element.84) | copy-start | bytes 1769476
  59.3 21.0 %collective-permute-start.12 = (bf16[4,96,768]{2,1,0:T(8,128)(2,1)}, bf16[4,96,768]{2,1,0:T(8,128)(2,1)S(1)}, u32[]{:S(2)}, u32[]{:S(2)}) collective-permute-start(bf16[4,96,768]{2,1,0:T(8,128)(2,1)} %get-tuple-element.84), channel_id=1, source_target_pairs={{0,16},{1,9},{2,18},{3,11},{4,20},{5,13},{6,22},{7,15},{8,24},{9,1... | collective-permute-start | bytes 1769480 | tf_op jit(solution)/shard_map/ppermute | solution.py:37
  76.6 2.2 copy-start.3
  79.7 11.3 %copy-start.5 = (bf16[512,768]{1,0:T(8,128)(2,1)}, bf16[512,768]{1,0:T(8,128)(2,1)S(1)}, u32[]{:S(2)}) copy-start(bf16[512,768]{1,0:T(8,128)(2,1)S(1)} %get-tuple-element.77.low_ref) | copy-start | bytes 2359300
  79.7 11.3 %copy-start.7 = (f32[512,768]{1,0:T(8,128)}, f32[512,768]{1,0:T(8,128)S(1)}, u32[]{:S(2)}) copy-start(f32[512,768]{1,0:T(8,128)S(1)} %get-tuple-element.83.normal_ref) | copy-start | bytes 4718596
  79.7 11.3 %copy-start.9 = (bf16[4,512,576]{2,1,0:T(8,128)(2,1)}, bf16[4,512,576]{2,1,0:T(8,128)(2,1)S(1)}, u32[]{:S(2)}) copy-start(bf16[4,512,576]{2,1,0:T(8,128)(2,1)S(1)} %get-tuple-element.91.qkv_ref) | copy-start | bytes 7077892
  79.7 4.8 %copy-start.2 = (f32[3072]{0:T(1024)S(1)}, f32[3072]{0:T(1024)}, u32[]{:S(2)}) copy-start(f32[3072]{0:T(1024)} %param.33) | copy-start | bytes 36868
  79.7 3.2 %collective-permute-start.10 = (bf16[8,96,768]{2,1,0:T(8,128)(2,1)S(1)}, bf16[8,96,768]{2,1,0:T(8,128)(2,1)S(1)}, u32[]{:S(2)}, u32[]{:S(2)}) collective-permute-start(bf16[8,96,768]{2,1,0:T(8,128)(2,1)S(1)} %pad_maximum_fusion.4.rest_0_), channel_id=1, source_target_pairs={{0,1},{1,0},{2,3},{3,2},{4,5},{5,4},{6,7},{7,6},{8,9},{9,8},{10,11... | collective-permute-start | bytes 3538952 | tf_op jit(solution)/shard_map/ppermute | solution.py:37
  79.9 4.6 %collective-permute-start.11 = (bf16[8,96,768]{2,1,0:T(8,128)(2,1)}, bf16[8,96,768]{2,1,0:T(8,128)(2,1)S(1)}, u32[]{:S(2)}, u32[]{:S(2)}) collective-permute-start(bf16[8,96,768]{2,1,0:T(8,128)(2,1)} %collective-permute-done.9.rest_1_), channel_id=1, source_target_pairs={{0,1},{1,0},{2,3},{3,2},{4,5},{5,4},{6,7},{7,6},{8,9},{9,8},{10,11... | collective-permute-start | bytes 3538952 | tf_op jit(solution)/shard_map/ppermute | solution.py:37
  80.4 16.3 %collective-permute-start.13 = (bf16[8,96,768]{2,1,0:T(8,128)(2,1)S(1)}, bf16[8,96,768]{2,1,0:T(8,128)(2,1)S(1)}, u32[]{:S(2)}, u32[]{:S(2)}) collective-permute-start(bf16[8,96,768]{2,1,0:T(8,128)(2,1)S(1)} %pad_maximum_fusion.5.rest_0_), channel_id=1, source_target_pairs={{0,2},{1,5},{2,0},{3,7},{4,6},{5,1},{6,4},{7,3},{8,10},{9,13},{10,... | collective-permute-start | bytes 3538952 | tf_op jit(solution)/shard_map/ppermute | solution.py:37
  84.5 12.7 %copy-start.18 = (f32[768]{0:T(1024)S(1)}, f32[768]{0:T(1024)}, u32[]{:S(2)}) copy-start(f32[768]{0:T(1024)} %param.35) | copy-start | bytes 9220
  84.5 12.7 %copy-start.19 = (f32[768]{0:T(1024)S(1)}, f32[768]{0:T(1024)}, u32[]{:S(2)}) copy-start(f32[768]{0:T(1024)} %param.36) | copy-start | bytes 9220
  84.5 12.7 %copy-start.20 = (f32[768]{0:T(1024)S(1)}, f32[768]{0:T(1024)}, u32[]{:S(2)}) copy-start(f32[768]{0:T(1024)} %param.37) | copy-start | bytes 9220
  84.6 16.7 %copy-start.1 = (bf16[512,768]{1,0:T(8,128)(2,1)S(1)}, bf16[512,768]{1,0:T(8,128)(2,1)}, u32[]{:S(2)}) copy-start(bf16[512,768]{1,0:T(8,128)(2,1)} %cotangent_ref.1) | copy-start | bytes 2359300
  96.7 2.8 %collective-permute-start.14 = (bf16[8,96,768]{2,1,0:T(8,128)(2,1)S(1)}, bf16[8,96,768]{2,1,0:T(8,128)(2,1)S(1)}, u32[]{:S(2)}, u32[]{:S(2)}) collective-permute-start(bf16[8,96,768]{2,1,0:T(8,128)(2,1)S(1)} %pad_maximum_fusion.5.rest_0_), channel_id=1, source_target_pairs={{0,1},{1,0},{2,3},{3,2},{4,5},{5,4},{6,7},{7,6},{8,9},{9,8},{10,11... | collective-permute-start | bytes 3538952 | tf_op jit(solution)/shard_map/ppermute | solution.py:37
  96.7 4.5 %collective-permute-start.15 = (bf16[8,96,768]{2,1,0:T(8,128)(2,1)S(1)}, bf16[8,96,768]{2,1,0:T(8,128)(2,1)S(1)}, u32[]{:S(2)}, u32[]{:S(2)}) collective-permute-start(bf16[8,96,768]{2,1,0:T(8,128)(2,1)S(1)} %collective-permute-done.13.rest_1_), channel_id=1, source_target_pairs={{0,1},{1,0},{2,3},{3,2},{4,5},{5,4},{6,7},{7,6},{8,9},{9,8},{10,11... | collective-permute-start | bytes 3538952 | tf_op jit(solution)/shard_map/ppermute | solution.py:37
  101.2 1.4 copy-start.8
  112.5 4.5 %collective-permute-start.16 = (bf16[16,96,768]{2,1,0:T(8,128)(2,1)S(1)}, bf16[16,96,768]{2,1,0:T(8,128)(2,1)S(1)}, u32[]{:S(2)}, u32[]{:S(2)}) collective-permute-start(bf16[16,96,768]{2,1,0:T(8,128)(2,1)S(1)} %get-tuple-element.98), channel_id=1, source_target_pairs={{0,1},{1,0},{2,3},{3,2},{4,5},{5,4},{6,7},{7,6},{8,9},{9,8},{10,11... | collective-permute-start | bytes 7077896 | tf_op jit(solution)/shard_map/ppermute | solution.py:37
  117.0 2.1 copy-start.6
  118.8 16.2 %collective-permute-start.17 = (bf16[8,96,768]{2,1,0:T(8,128)(2,1)S(1)}, bf16[8,96,768]{2,1,0:T(8,128)(2,1)S(1)}, u32[]{:S(2)}, u32[]{:S(2)}) collective-permute-start(bf16[8,96,768]{2,1,0:T(8,128)(2,1)S(1)} %get-tuple-element.181), channel_id=1, source_target_pairs={{0,2},{1,5},{2,0},{3,7},{4,6},{5,1},{6,4},{7,3},{8,10},{9,13},{10,... | collective-permute-start | bytes 3538952 | tf_op jit(solution)/shard_map/ppermute | solution.py:37
  135.0 4.5 %collective-permute-start.18 = (bf16[16,96,768]{2,1,0:T(8,128)(2,1)S(1)}, bf16[16,96,768]{2,1,0:T(8,128)(2,1)S(1)}, u32[]{:S(2)}, u32[]{:S(2)}) collective-permute-start(bf16[16,96,768]{2,1,0:T(8,128)(2,1)S(1)} %get-tuple-element.106), channel_id=1, source_target_pairs={{0,1},{1,0},{2,3},{3,2},{4,5},{5,4},{6,7},{7,6},{8,9},{9,8},{10,11... | collective-permute-start | bytes 7077896 | tf_op jit(solution)/shard_map/ppermute | solution.py:37
  140.3 23.2 %collective-permute-start.20 = (bf16[8,96,768]{2,1,0:T(8,128)(2,1)S(1)}, bf16[8,96,768]{2,1,0:T(8,128)(2,1)S(1)}, u32[]{:S(2)}, u32[]{:S(2)}) collective-permute-start(bf16[8,96,768]{2,1,0:T(8,128)(2,1)S(1)} %get-tuple-element.179), channel_id=1, source_target_pairs={{0,2},{1,5},{2,0},{3,7},{4,6},{5,1},{6,4},{7,3},{8,10},{9,13},{10,... | collective-permute-start | bytes 3538952 | tf_op jit(solution)/shard_map/ppermute | solution.py:37
  140.8 1.7 copy-start.10
  140.8 1.9 copy-start.12
  141.1 22.4 %collective-permute-start.19 = (bf16[4,96,768]{2,1,0:T(8,128)(2,1)S(1)}, bf16[4,96,768]{2,1,0:T(8,128)(2,1)S(1)}, u32[]{:S(2)}, u32[]{:S(2)}) collective-permute-start(bf16[4,96,768]{2,1,0:T(8,128)(2,1)S(1)} %get-tuple-element.115), channel_id=1, source_target_pairs={{0,16},{1,9},{2,18},{3,11},{4,20},{5,13},{6,22},{7,15},{8,24},{9,1... | collective-permute-start | bytes 1769480 | tf_op jit(solution)/shard_map/ppermute | solution.py:37
  142.7 2.3 %copy-start.4 = (bf16[4,768,768]{2,1,0:T(8,128)(2,1)S(1)}, bf16[4,768,768]{2,1,0:T(8,128)(2,1)}, u32[]{:S(2)}) copy-start(bf16[4,768,768]{2,1,0:T(8,128)(2,1)} %copy-done.3) | copy-start | bytes 14155780
  163.5 5.7 %collective-permute-start.21 = (bf16[16,112,768]{2,1,0:T(8,128)(2,1)S(1)}, bf16[16,112,768]{2,1,0:T(8,128)(2,1)S(1)}, u32[]{:S(2)}, u32[]{:S(2)}) collective-permute-start(bf16[16,112,768]{2,1,0:T(8,128)(2,1)S(1)} %get-tuple-element.116), channel_id=1, source_target_pairs={{0,1},{1,0},{2,3},{3,2},{4,5},{5,4},{6,7},{7,6},{8,9},{9,8},{10,11... | collective-permute-start | bytes 8257544 | tf_op jit(solution)/shard_map/ppermute | solution.py:37
  170.2 18.6 %collective-permute-start.22 = (bf16[8,112,768]{2,1,0:T(8,128)(2,1)S(1)}, bf16[8,112,768]{2,1,0:T(8,128)(2,1)S(1)}, u32[]{:S(2)}, u32[]{:S(2)}) collective-permute-start(bf16[8,112,768]{2,1,0:T(8,128)(2,1)S(1)} %pad_maximum_fusion.1), channel_id=1, source_target_pairs={{0,2},{1,5},{2,0},{3,7},{4,6},{5,1},{6,4},{7,3},{8,10},{9,13},{10,... | collective-permute-start | bytes 4128776 | tf_op jit(solution)/shard_map/ppermute | solution.py:37
  171.6 17.2 %collective-permute-start.23 = (bf16[4,96,768]{2,1,0:T(8,128)(2,1)S(1)}, bf16[4,96,768]{2,1,0:T(8,128)(2,1)S(1)}, u32[]{:S(2)}, u32[]{:S(2)}) collective-permute-start(bf16[4,96,768]{2,1,0:T(8,128)(2,1)S(1)} %get-tuple-element.189), channel_id=1, source_target_pairs={{0,16},{1,9},{2,18},{3,11},{4,20},{5,13},{6,22},{7,15},{8,24},{9,1... | collective-permute-start | bytes 1769480 | tf_op jit(solution)/shard_map/ppermute | solution.py:37
  189.8 23.5 %collective-permute-start.24 = (bf16[4,112,768]{2,1,0:T(8,128)(2,1)S(1)}, bf16[4,112,768]{2,1,0:T(8,128)(2,1)S(1)}, u32[]{:S(2)}, u32[]{:S(2)}) collective-permute-start(bf16[4,112,768]{2,1,0:T(8,128)(2,1)S(1)} %pad_maximum_fusion.7), channel_id=1, source_target_pairs={{0,16},{1,9},{2,18},{3,11},{4,20},{5,13},{6,22},{7,15},{8,24},{9,1... | collective-permute-start | bytes 2064392 | tf_op jit(solution)/shard_map/ppermute | solution.py:37
  191.0 9.9 %collective-permute-start.25 = (bf16[2,2,96,768]{3,2,0,1:T(8,128)(2,1)S(1)}, bf16[2,2,96,768]{3,2,0,1:T(8,128)(2,1)S(1)}, u32[]{:S(2)}, u32[]{:S(2)}) collective-permute-start(bf16[2,2,96,768]{3,2,0,1:T(8,128)(2,1)S(1)} %pad_maximum_fusion.10), channel_id=1, source_target_pairs={{0,4},{1,3},{2,6},{3,1},{4,0},{5,7},{6,2},{7,5},{8,12},{9,11},{10,... | collective-permute-start | bytes 1769480 | tf_op jit(solution)/shard_map/ppermute | solution.py:37
  213.6 7.3 %collective-permute-start.28 = (bf16[1,2,96,768]{3,2,0,1:T(8,128)(2,1)S(1)}, bf16[1,2,96,768]{3,2,0,1:T(8,128)(2,1)S(1)}, u32[]{:S(2)}, u32[]{:S(2)}) collective-permute-start(bf16[1,2,96,768]{3,2,0,1:T(8,128)(2,1)S(1)} %add_convert_fusion.8), channel_id=1, source_target_pairs={{0,8},{1,17},{2,10},{3,19},{4,12},{5,21},{6,14},{7,23},{8,0},{9,25... | collective-permute-start | bytes 884744 | tf_op jit(solution)/shard_map/ppermute | solution.py:37
  213.8 8.1 %collective-permute-start.26 = (bf16[2,112,768]{2,1,0:T(8,128)(2,1)S(1)}, bf16[2,112,768]{2,1,0:T(8,128)(2,1)S(1)}, u32[]{:S(2)}, u32[]{:S(2)}) collective-permute-start(bf16[2,112,768]{2,1,0:T(8,128)(2,1)S(1)} %pad_maximum_fusion.12), channel_id=1, source_target_pairs={{0,4},{1,3},{2,6},{3,1},{4,0},{5,7},{6,2},{7,5},{8,12},{9,11},{10,... | collective-permute-start | bytes 1032200 | tf_op jit(solution)/shard_map/ppermute | solution.py:37
  222.1 5.5 %collective-permute-start.27 = (bf16[1,112,768]{2,1,0:T(8,128)(2,1)S(1)}, bf16[1,112,768]{2,1,0:T(8,128)(2,1)S(1)}, u32[]{:S(2)}, u32[]{:S(2)}) collective-permute-start(bf16[1,112,768]{2,1,0:T(8,128)(2,1)S(1)} %pad_maximum_fusion.15), channel_id=1, source_target_pairs={{0,8},{1,17},{2,10},{3,19},{4,12},{5,21},{6,14},{7,23},{8,0},{9,25... | collective-permute-start | bytes 516104 | tf_op jit(solution)/shard_map/ppermute | solution.py:37
  (2 other events, 2.1 us)

commit v2 on v1

v2 whole, which is shorter than its diff:
```python
from functools import partial
import math

import jax
import jax.numpy as jnp
import numpy as np
from jax import lax
from jax.experimental import pallas as pl
from jax.experimental.pallas import tpu as pltpu
from jax.sharding import PartitionSpec as P

HD = 64
SEQ = 512
AXES = ("fsdp", "tp")
F32 = jnp.float32
BF16 = jnp.bfloat16
CUTS = 8
MIB = 1 << 20


def exchange_plan(fsdp, tp):
    count = fsdp * tp
    if (fsdp, tp) == (8, 4):
        select, pairs = 1, [(8, 16), (4, 2), (16, 8), (2, 4)]
    else:
        select = tp
        pairs = [(1 << i,) * 2 for i in range(count.bit_length() - 1) if 1 << i != select]
    steps = [[d ^ pair[1 if d & select else 0] for d in range(count)] for pair in pairs]
    steps.append([d ^ select for d in range(count)])
    sources = [[d] for d in range(count)]
    for step in steps:
        sources = [sources[d] + sources[step[d]] for d in range(count)]
    return steps, np.array(sources)


def swap(array, step):
    return lax.ppermute(array, AXES, list(enumerate(step)))


def after(array, *others):
    return lax.optimization_barrier((array, *others))[0]


class Gather:
    def __init__(self, shard, steps):
        self.steps, self.at, self.held, self.pieces = steps, 0, shard[None], None

    def step(self, *others):
        step = self.steps[self.at]
        self.at += 1
        if others:
            self.held = after(self.held, *others)
        moved = swap(self.held, step)
        if self.at == len(self.steps) - 1:
            self.pieces = [self.held, moved]
        else:
            self.held = jnp.concatenate([self.held, moved], axis=0)
        return moved

    def split(self):
        parts = []
        for i in range(self.held.shape[1]):
            part = Gather(self.held[0, i], self.steps)
            part.at, part.held = self.at, self.held[:, i]
            parts.append(part)
        return parts

    def finish(self, *others):
        pieces = [after(piece, *others) for piece in self.pieces] if others else self.pieces
        return self.pieces + [swap(piece, self.steps[-1]) for piece in pieces]


class Sum:
    def __init__(self, keep, send, steps, extra=0):
        self.steps, self.at, self.keep, self.send, self.extra = steps, len(steps) - 1, keep, send, extra

    def add(self, keep, moved):
        keep, moved = keep.astype(F32), moved.astype(F32)
        if not self.extra:
            return keep + moved
        rows = keep.shape[1] - 2 * self.extra
        total = (keep + moved)[:, :rows]
        high = slice(rows, rows + self.extra)
        low = slice(rows + self.extra, None)
        side = (keep[:, high] + keep[:, low]) + (moved[:, high] + moved[:, low])
        if self.at == 0:
            return total, side
        high = lax.reduce_precision(side, 8, 7)
        return jnp.concatenate([total, high, side - high], axis=1)

    def start(self, *others):
        send = after(self.send, *others) if others else self.send
        half = send.shape[0] // 2
        parts = [send[:half], send[half:]] if self.at == len(self.steps) - 1 else [send]
        self.moved = [swap(part, self.steps[self.at]) for part in parts]

    def hold(self, *others):
        self.moved = list(lax.optimization_barrier((*self.moved, *others))[: len(self.moved)])

    def end(self):
        if self.at == 0:
            return self.add(self.keep, self.moved[0])
        half = self.keep.shape[0] // 2
        if len(self.moved) == 1:
            moved = self.moved[0][:half], self.moved[0][half:]
        else:
            moved = self.moved
        send = self.add(self.keep[half:], moved[1]).astype(BF16)
        keep = self.add(self.keep[:half], moved[0]).astype(BF16)
        self.keep, self.send = keep, send
        self.at -= 1
        return send

    def step(self, *others):
        self.start(*others)
        return self.end()

    @staticmethod
    def merge(*packages):
        one = packages[0]
        keep, send = (
            jnp.stack([getattr(package, name) for package in packages], axis=1) for name in ("keep", "send")
        )
        merged = Sum(keep, send, one.steps)
        merged.at = one.at
        return merged


def both(*packages):
    moved = lax.optimization_barrier([package.moved for package in packages])
    for package, arrived in zip(packages, moved):
        package.moved = arrived
        package.end()


def copy_block(order_ref, from_ref, to_ref):
    to_ref[...] = from_ref[...]


def laid_out(blocks, slot_of, fsdp, tp):
    _, rows, cols = blocks.shape
    grid_spec = pltpu.PrefetchScalarGridSpec(
        num_scalar_prefetch=1,
        grid=(fsdp, tp),
        in_specs=[pl.BlockSpec((1, rows, cols), lambda f, t, s: (s[f * tp + t], 0, 0))],
        out_specs=pl.BlockSpec((1, rows, cols), lambda f, t, s: (f, 0, t)),
    )
    return pl.pallas_call(
        copy_block,
        grid_spec=grid_spec,
        out_shape=jax.ShapeDtypeStruct((fsdp, rows, tp * cols), blocks.dtype),
    )(slot_of, blocks)


def cut_up(full, slot_of, fsdp, tp):
    _, rows, cols = full.shape
    cols = cols // tp
    grid_spec = pltpu.PrefetchScalarGridSpec(
        num_scalar_prefetch=1,
        grid=(fsdp, tp),
        in_specs=[pl.BlockSpec((1, rows, cols), lambda f, t, s: (f, 0, t))],
        out_specs=pl.BlockSpec((1, rows, cols), lambda f, t, s: (s[f * tp + t], 0, 0)),
    )
    return pl.pallas_call(
        copy_block,
        grid_spec=grid_spec,
        out_shape=jax.ShapeDtypeStruct((fsdp * tp, rows, cols), full.dtype),
    )(slot_of, full)


def dot(a, b):
    return lax.dot_general(a, b, (((1,), (0,)), ((), ())), preferred_element_type=F32)


def dot_nt(a, b):
    return lax.dot_general(a, b, (((1,), (1,)), ((), ())), preferred_element_type=F32)


def dot_tn(a, b):
    return lax.dot_general(a, b, (((0,), (0,)), ((), ())), preferred_element_type=F32)


def norm_forward(values):
    average = jnp.mean(values, axis=-1, keepdims=True)
    centered = values - average
    inverse = lax.rsqrt(jnp.mean(centered * centered, axis=-1, keepdims=True) + 1e-12)
    return centered * inverse, inverse


def norm_backward(upstream, normal, inverse, gain):
    scaled = upstream * gain
    return inverse * (
        scaled
        - jnp.mean(scaled, axis=-1, keepdims=True)
        - normal * jnp.mean(scaled * normal, axis=-1, keepdims=True)
    )


def gelu_parts(x):
    below = 0.5 + 0.5 * lax.erf(x * math.sqrt(0.5))
    return x * below, below + x * (jnp.exp(-0.5 * (x * x)) * (1.0 / math.sqrt(2.0 * math.pi)))


def column_sum(array):
    return jnp.sum(array, axis=0, keepdims=True)


def assemble(half, place_ref, pieces, weight):
    rows = weight.shape[1] // CUTS
    per = pieces[0].shape[0]
    count = per * len(pieces)
    for slot in range(count):
        place = place_ref[half * count + slot]
        i = place // CUTS
        cut = place - i * CUTS
        weight[i, pl.ds(pl.multiple_of(cut * rows, rows), rows), :] = pieces[slot // per][slot % per]


def put_blocks(half, slot_ref, out_ref, i, value, cols=slice(None)):
    rows = value.shape[0] // CUTS
    for cut in range(CUTS):
        slot = slot_ref[half * out_ref.shape[0] + i * CUTS + cut]
        out_ref[slot, :rows, cols] = value[cut * rows : (cut + 1) * rows].astype(out_ref.dtype)


def each(count, step):
    lax.fori_loop(0, count, lambda i, carry: (step(i), carry)[1], 0)


def attention_kernel(half, place_ref, turn_ref, tokens_ref, ids_row, ids_col, bias_ref, *rest):
    if half == 0:
        output_bias, *rest = rest
        *pieces, weight, qkv_ref, context_ref, exponent_ref, total_ref, acc, turned_ref, mask = rest
        acc[...] = tokens_ref[...].astype(F32) + output_bias[...]
        turned_ref[...] = tokens_ref[...].T
    else:
        acc_ref, gain, shift, *rest = rest
        *pieces, weight, qkv_ref, context_ref, exponent_ref, total_ref = rest[:-5]
        normal_ref, inverse_ref, low_ref, mask, acc = rest[-5:]
        acc[...] = acc_ref[...]
    cols = context_ref.shape[1]
    count = weight.shape[0]
    assemble(half, place_ref, pieces, weight)
    mask[...] = jnp.where(ids_col[...] == ids_row[...], 0.0, -1e30)

    def step(i):
        bias = bias_ref[turn_ref[half * count + i]]
        qkv = (dot(tokens_ref[...], weight[i, :, : 3 * cols]) + bias).astype(BF16)
        qkv_ref[i] = qkv
        contexts = []
        for h in range(cols // HD):
            queries, keys, values = (
                qkv[:, part * cols + h * HD : part * cols + (h + 1) * HD] for part in range(3)
            )
            scores = dot_nt(keys, queries * (HD**-0.5)) + mask[...]
            top = jnp.max(scores, axis=0, keepdims=True)
            exponent = jnp.exp(scores - top)
            total = 1.0 / jnp.sum(exponent, axis=0, keepdims=True)
            exponent = exponent.astype(BF16)
            exponent_ref[i, h] = exponent
            contexts.append((dot_tn(values, exponent) * total).astype(BF16))
            total_ref[i, h : h + 1] = total
        context = jnp.concatenate(contexts, axis=0)
        context_ref[i] = context
        acc[...] += dot_nt(context.T, weight[i, :, 3 * cols :])

    each(count, step)
    if half == 1:
        normal, inverse = norm_forward(acc[...])
        normal_ref[...] = normal
        inverse_ref[...] = inverse
        low_ref[...] = (normal * gain[...] + shift[...]).astype(BF16)


def up_kernel(place_ref, turn_ref, low_ref, bias_ref, *rest):
    *pieces, weight_first, active_first, slope_first, weight_second, active_second, slope_second = rest
    many = len(pieces) // 2
    up_half(0, place_ref, turn_ref, low_ref, bias_ref, pieces[:many], weight_first, active_first, slope_first)
    up_half(1, place_ref, turn_ref, low_ref, bias_ref, pieces[many:], weight_second, active_second, slope_second)


def up_half(half, place_ref, turn_ref, low_ref, bias_ref, pieces, weight, active_ref, slope_ref):
    count = weight.shape[0]
    assemble(half, place_ref, pieces, weight)

    def step(i):
        pre = dot(low_ref[...], weight[i]) + bias_ref[turn_ref[half * count + i]]
        active, slope = gelu_parts(pre)
        active_ref[i] = active.astype(BF16)
        slope_ref[i] = slope.astype(BF16)

    each(count, step)


def down_first_kernel(place_ref, active_ref, normal_ref, first_gain, first_shift, bias_ref, *rest):
    *pieces, weight, acc = rest
    assemble(0, place_ref, pieces, weight)
    acc[...] = normal_ref[...] * first_gain[...] + (first_shift[...] + bias_ref[...])

    def step(i):
        acc[...] += dot_nt(active_ref[i], weight[i])

    each(weight.shape[0], step)


def down_second_kernel(place_ref, slot_ref, active_ref, acc_ref, gain, shift, cotangent_ref, *rest):
    *pieces, weight, output_ref, grad_ref, low_ref, turned_ref, sums_ref, send_ref, acc = rest
    count = weight.shape[0]
    assemble(1, place_ref, pieces, weight)
    acc[...] = acc_ref[...]

    def step(i):
        acc[...] += dot_nt(active_ref[i], weight[i])

    each(count, step)
    normal, inverse = norm_forward(acc[...])
    output_ref[...] = normal * gain[...] + shift[...]
    upstream = cotangent_ref[...].astype(F32)
    grad = norm_backward(upstream, normal, inverse, gain[...])
    grad_ref[...] = grad
    low = grad.astype(BF16)
    low_ref[...] = low
    turned_ref[...] = low.T
    sums_ref[0:1] = column_sum(grad)
    sums_ref[1:2] = column_sum(upstream * normal)
    sums_ref[2:3] = column_sum(upstream)
    each(count, lambda i: put_blocks(1, slot_ref, send_ref, i, dot(turned_ref[...], active_ref[i])))


def down_third_kernel(slot_ref, active_ref, turned_ref, keep_ref):
    each(
        active_ref.shape[0],
        lambda i: put_blocks(0, slot_ref, keep_ref, i, dot(turned_ref[...], active_ref[i])),
    )


def middle_kernel(half, slot_ref, low_grad_ref, slope_ref, *rest):
    if half == 1:
        grad_ref, low_ref, up_w, down_w, out_ref, sums_ref, acc, turned = rest
        acc[...] = grad_ref[...]
        turned[...] = low_ref[...].T
    else:
        acc_ref, turned, normal_ref, inverse_ref, gain, up_w, down_w, *rest = rest
        out_ref, sums_ref, resid_ref, resid_low_ref, resid_turned_ref, acc = rest
        acc[...] = acc_ref[...]

    def step(i):
        wide = dot(low_grad_ref[...], down_w[i]) * slope_ref[i].astype(F32)
        pre_grad = wide.astype(BF16)
        sums_ref[pl.ds(3 + i, 1)] = column_sum(wide)
        put_blocks(half, slot_ref, out_ref, i, dot(turned[...], pre_grad))
        acc[...] += dot_nt(pre_grad, up_w[i])

    each(up_w.shape[0], step)
    if half == 0:
        grad_one = acc[...]
        normal = normal_ref[...]
        resid = norm_backward(grad_one, normal, inverse_ref[...], gain[...])
        resid_ref[...] = resid
        low = resid.astype(BF16)
        resid_low_ref[...] = low
        resid_turned_ref[...] = low.T
        sums_ref[0:1] = column_sum(resid)
        sums_ref[1:2] = column_sum(grad_one * normal)
        sums_ref[2:3] = column_sum(grad_one)


def attention_back_kernel(slot_ref, turned_ref, resid_ref, resid_low_ref, resid_turned_ref, *rest):
    *parts, grad_ref, sums_second, sums_first, send_ref, keep_ref = rest
    grad_ref[...] = resid_ref[...]
    many = len(parts) // 2
    shared = (slot_ref, turned_ref, resid_low_ref, resid_turned_ref, grad_ref)
    attention_back(1, *shared, *parts[:many], sums_second, send_ref)
    attention_back(0, *shared, *parts[many:], sums_first, keep_ref)


def attention_back(
    half, slot_ref, turned_ref, resid_low_ref, resid_turned_ref, grad_ref, sums_in_ref, qkv_ref, context_ref,
    exponent_ref, total_ref, weight, sums_ref, out_ref,
):
    cols = context_ref.shape[1]
    factor = HD**-0.5
    extra = sums_ref.shape[1]
    main = out_ref.shape[1] - 2 * extra

    def step(i):
        outer = dot(resid_low_ref[...], weight[i, :, 3 * cols :])
        totals = total_ref[i].T
        query_grads, key_grads, value_grads = [], [], []
        for h in range(cols // HD):
            at = slice(h * HD, (h + 1) * HD)
            queries, keys, values = (
                qkv_ref[i, :, part * cols + h * HD : part * cols + (h + 1) * HD] for part in range(3)
            )
            queries = queries * factor
            upstream = (outer[:, at] * totals[:, h : h + 1]).astype(BF16)
            row_term = jnp.sum(
                upstream.T.astype(F32) * context_ref[i, at].astype(F32), axis=0, keepdims=True
            )
            exponent = exponent_ref[i, h]
            prob_grad = dot_nt(values, upstream)
            score_grad = (exponent.astype(F32) * (prob_grad - row_term)).astype(BF16)
            key_grads.append(dot(score_grad, queries).astype(BF16))
            value_grads.append(dot(exponent, upstream).astype(BF16))
            query_grads.append((dot_tn(keys, score_grad) * factor).astype(BF16))
        queries = jnp.concatenate(query_grads, axis=0).T
        grad = jnp.concatenate([queries, *key_grads, *value_grads], axis=1)
        grad_ref[...] += dot_nt(grad, weight[i, :, : 3 * cols])
        put_blocks(half, slot_ref, out_ref, i, dot(turned_ref[...], grad), slice(0, 3 * cols))
        out_grad = dot_nt(resid_turned_ref[...], context_ref[i])
        put_blocks(half, slot_ref, out_ref, i, out_grad, slice(3 * cols, None))
        columns = column_sum(grad.astype(F32))
        side = jnp.concatenate([columns, jnp.zeros((1, cols), F32)], axis=1)
        side = jnp.concatenate([sums_in_ref[i], side], axis=0)
        sums_ref[i] = side
        high = side.astype(BF16)
        low = (side - high.astype(F32)).astype(BF16)
        side = jnp.concatenate([high, low], axis=0)
        for cut in range(CUTS):
            out_ref[slot_ref[half * out_ref.shape[0] + i * CUTS + cut], main:, :] = side

    each(weight.shape[0], step)


def call(kernel, pieces, scalars, inputs, outs, scratch, flops, limit=16):
    whole = pl.BlockSpec(memory_space=pltpu.VMEM)
    smem = pl.BlockSpec(memory_space=pltpu.SMEM)
    return pl.pallas_call(
        kernel,
        in_specs=[smem] * len(scalars) + [whole] * len(inputs) + [whole] * len(pieces),
        out_specs=[whole] * len(outs),
        out_shape=[jax.ShapeDtypeStruct(*out) for out in outs],
        scratch_shapes=scratch,
        compiler_params=pltpu.CompilerParams(vmem_limit_bytes=limit * MIB),
        cost_estimate=pl.CostEstimate(flops=1024, bytes_accessed=1024, transcendentals=0),
    )(*scalars, *inputs, *pieces)


def shards(
    steps,
    sources,
    fsdp,
    tp,
    tokens,
    segment_ids,
    query_weight,
    key_weight,
    value_weight,
    query_bias,
    value_bias,
    output_weight,
    output_bias,
    first_gain,
    first_shift,
    up_weight,
    up_bias,
    down_weight,
    down_bias,
    second_gain,
    second_shift,
    cotangent,
):
    rows, cols = query_weight.shape
    width = rows * fsdp
    units = up_weight.shape[1]
    count = fsdp * tp
    cut_rows = width // CUTS
    blocks_n = CUTS * tp
    direct = blocks_n == count
    place = lax.axis_index("tp")
    me = lax.axis_index("fsdp") * tp + place
    doc_ids = lax.dynamic_slice_in_dim(segment_ids, place * SEQ, SEQ)

    def mine(table):
        return lax.dynamic_index_in_dim(jnp.asarray(table, jnp.int32), me, keepdims=False)

    slot_of = mine(np.argsort(sources, axis=1))
    kept = tp // 2
    if direct:
        sides = np.array(sources).reshape(count, 2, -1) % tp
        columns = np.sort(np.array([[np.unique(part) for part in parts] for parts in sides]), axis=2)
        inner = (sides[..., None] == columns[:, :, None, :]).argmax(axis=-1)
        spots = inner * CUTS + np.array(sources).reshape(count, 2, -1) // tp
        places = mine(spots.reshape(count, -1))
        slots = mine(np.argsort(spots, axis=2).reshape(count, -1))
        turns = mine(columns.reshape(count, -1))
    else:
        places = slots = jnp.tile(jnp.arange(blocks_n // 2, dtype=jnp.int32), 2)
        turns = jnp.arange(tp, dtype=jnp.int32)

    def ready(pieces):
        if direct:
            return pieces
        full = laid_out(jnp.concatenate(pieces, axis=0), slot_of, fsdp, tp)
        full = full.reshape(CUTS, cut_rows, tp, -1).transpose(2, 0, 1, 3)
        full = full.reshape(2, blocks_n // 2, cut_rows, -1)
        return [full[0], full[1]]

    def outgoing(keep, send, extra=0):
        if direct:
            return Sum(keep, send, steps, extra)
        blocks = jnp.concatenate([keep, send], axis=0)[:, :cut_rows]
        full = blocks.reshape(tp, CUTS, cut_rows, -1).transpose(1, 2, 0, 3)
        blocks = cut_up(full.reshape(fsdp, rows, -1), slot_of, fsdp, tp)
        return Sum(blocks[: count // 2], blocks[count // 2 :], steps)

    query_bias, value_bias = query_bias.reshape(tp, 1, cols), value_bias.reshape(tp, 1, cols)
    blank = jnp.zeros_like(query_bias)
    qkv_bias = jnp.concatenate([query_bias, blank, value_bias], axis=2)
    up_bias = up_bias.reshape(tp, 1, units)
    vectors = jnp.stack(
        [output_bias, first_gain, first_shift, down_bias, second_gain, second_shift]
    ).reshape(6, 1, width)
    output_bias, first_gain, first_shift, down_bias, second_gain, second_shift = (
        vectors[i] for i in range(6)
    )
    ids_row, ids_col = doc_ids.reshape(1, -1), doc_ids.reshape(-1, 1)

    a = Gather(jnp.concatenate([query_weight, key_weight, value_weight, output_weight.T], axis=1), steps)
    b = Gather(up_weight, steps)
    c = Gather(down_weight.T, steps)
    if direct:
        pair = Gather(jnp.stack([up_weight, down_weight.T]), steps)
        first = a.step()
        pair.held = after(pair.held, first)
        a_x = a.step(qkv_bias, up_bias, vectors, ids_row, ids_col)
        pair.step()
        a.held, pair.held = lax.optimization_barrier((a.held, pair.held))
        a.step()
        pair.step()
        a.held, pair.held = lax.optimization_barrier((a.held, pair.held))
        b, c = pair.split()
        a_x = a.step()
        b_z = b.step()
        a.pieces, b.held = lax.optimization_barrier((a.pieces, b.held))
        attn_w = ready(a.finish())
        b_x = b.step()
        c_z = c.step(b_z)
    else:
        for package in (a, b, c):
            for _ in steps[:-1]:
                package.step()
        attn_w = ready(a.finish())
    many = len(attn_w) // 2
    parts = kept
    weight = ((parts, width, units), BF16)
    half = ((blocks_n // 2, cut_rows, units), BF16)
    side_half = ((blocks_n // 2, cut_rows + 16, units), BF16)
    state = pltpu.VMEM((SEQ, width), F32)
    turned = pltpu.VMEM((width, SEQ), BF16)
    mask = pltpu.VMEM((SEQ, SEQ), F32)
    wide, narrow = (SEQ, width), ((SEQ, width), BF16)
    full = (wide, F32)
    flipped = ((width, SEQ), BF16)
    flops = 2 * SEQ * width * width
    kept_outs = [weight, ((parts, SEQ, 3 * cols), BF16), ((parts, cols, SEQ), BF16),
                 ((parts, cols // HD, SEQ, SEQ), BF16), ((parts, 8, SEQ), F32)]
    common = (tokens, ids_row, ids_col, qkv_bias)
    *attn_first, acc, tokens_turned = call(
        partial(attention_kernel, 0), attn_w[:many], (places, turns), (*common, output_bias),
        [*kept_outs, full, flipped], [mask], 4 * flops,
    )
    *attn_second, normal, inverse, low = call(
        partial(attention_kernel, 1), attn_w[many:], (places, turns), (*common, acc, first_gain, first_shift),
        [*kept_outs, full, ((SEQ, 1), F32), narrow], [mask, state], 4 * flops,
    )
    if direct:
        up_w = b.finish(inverse)
        c.step(inverse, b_x)
    else:
        up_w = ready(b.finish())
    outs = [weight, ((parts, SEQ, units), BF16), ((parts, SEQ, units), BF16)]
    up_first, active_first, slope_first, up_second, active_second, slope_second = call(
        up_kernel, up_w, (places, turns), (low, up_bias), outs * 2, [], 6 * flops
    )
    down_w = c.finish(slope_second) if direct else ready(c.finish())
    down_first, acc = call(
        down_first_kernel, down_w[:many], (places,),
        (active_first, normal, first_gain, first_shift, down_bias), [weight, full], [], 2 * flops,
    )
    down_second, layer_output, grad_two, grad_low, grad_turned, down_sums, down_send = call(
        down_second_kernel, down_w[many:], (places, slots),
        (active_second, acc, second_gain, second_shift, cotangent),
        [weight, full, full, narrow, flipped, ((8, width), F32), half], [state], 5 * flops,
    )
    (down_keep,) = call(
        down_third_kernel, [], (slots,), (active_first, grad_turned), [half], [], 2 * flops
    )
    down_sum = outgoing(down_keep, down_send)
    if direct:
        first = down_sum.step()
        down_sum.start()
        grad_low = after(grad_low, first)
    up_send, sums_second, acc, low_turned = call(
        partial(middle_kernel, 1), [up_second, down_second], (slots,),
        (grad_low, slope_second, grad_two, low), [half, ((8, width), F32), full, flipped], [], 6 * flops,
    )
    up_keep, sums_first, resid, resid_low, resid_turned = call(
        partial(middle_kernel, 0), [up_first, down_first], (slots,),
        (grad_low, slope_first, acc, low_turned, normal, inverse, first_gain),
        [half, ((8, width), F32), full, narrow, flipped], [state], 6 * flops,
    )
    up_sum = outgoing(up_keep, up_send)
    if direct:
        moved = down_sum.moved
        sent = down_sum.end()
        down_sum.start(sums_first)
        up_sum.start()
        up_sum.hold(resid_low, sent)
        first = up_sum.end()
        up_sum.start()
        resid_low = after(resid_low, first, sent)
    shared = jnp.concatenate([down_sums[:3], sums_first[:3]], axis=0)[None]

    def with_units(sums):
        return jnp.concatenate([jnp.broadcast_to(shared, (parts, 6, width)), sums[3 : 3 + parts, None]], axis=1)

    weight_second, *attn_second = attn_second
    weight_first, *attn_first = attn_first
    side_sums = ((parts, 8, units), F32)
    input_grad, side_second, side_first, attn_send, attn_keep = call(
        attention_back_kernel, [], (slots,),
        (tokens_turned, resid, resid_low, resid_turned, with_units(sums_second), *attn_second, weight_second,
         with_units(sums_first), *attn_first, weight_first),
        [full, side_sums, side_sums, side_half, side_half], [], 20 * flops,
    )
    attn_sum = outgoing(attn_keep, attn_send, 8)
    if direct:
        attn_sum.step(*down_sum.moved, *up_sum.moved)
        down_sum.end()
        up_sum.end()
        attn_sum.start()
        up_sum.start()
        both(attn_sum, up_sum)
        pair = Sum.merge(down_sum, up_sum)
        attn_sum.start()
        pair.start()
        both(attn_sum, pair)
        attn_sum.start()
        pair.start()
        attn_sum.end()
        finals = [[part] for part in pair.end()[0]]
        attn_sum.start()
        finals.append(attn_sum.end())
    else:
        side = jnp.concatenate([side_first, side_second], axis=0)
        finals = []
        for package in (down_sum, up_sum, attn_sum):
            while package.at > 0:
                package.step()
            package.start()
            finals.append(package.end())
    if direct:
        attn_grad, side = finals[2][0][0], finals[2][1][0]
    else:
        attn_grad = finals[2][0]
        side = lax.dynamic_index_in_dim(lax.psum(side, AXES), place, keepdims=False)
    return (
        layer_output,
        input_grad,
        attn_grad[:, :cols],
        attn_grad[:, cols : 2 * cols],
        attn_grad[:, 2 * cols : 3 * cols],
        side[7, :cols],
        side[7, 2 * cols : 3 * cols],
        attn_grad[:, 3 * cols :].T,
        side[3],
        side[4],
        side[5],
        finals[1][0],
        side[6],
        finals[0][0].T,
        side[0],
        side[1],
        side[2],
    )


def solution(mesh):
    fsdp, tp = mesh.shape["fsdp"], mesh.shape["tp"]
    steps, sources = exchange_plan(fsdp, tp)
    both, up, down = P(AXES, None), P("fsdp", "tp"), P("tp", "fsdp")
    return jax.shard_map(
        partial(shards, steps, sources, fsdp, tp),
        mesh=mesh,
        in_specs=(
            both, P("fsdp"), up, up, up, P(), P(), down, P(), P(), P(), up, P(), down, P(), P(), P(), both,
        ),
        out_specs=(
            both, both, up, up, up, P("tp"), P("tp"), down, P(), P(), P(), up, P("tp"), down, P(), P(), P(),
        ),
        check_vma=False,
    )
```

time: 232 us -> 217 us (0.935)
  waiting for transfers between devices: 114 us -> 99.8 us
  local copies, waits for them, and re-layouts: 17.4 us -> 11.6 us
  Pallas kernels: 59.6 us -> 63.5 us
    ppermute x29 -> x32, waiting for transfers between devices: 114 us -> 99.8 us  [swap(): return lax.ppermute(array, AXES, list(enumerate(step)))]
    unnamed x44 -> x40, local copies, waits for them, and re-layouts: 9.01 us -> 2.75 us
    pallas_call x5 -> x9, Pallas kernels: 59.6 us -> 63.5 us  [call(): pl.pallas_call(kernel, in_specs=[smem] * len(scalars) + [whole] * len(inp...]
    ppermute x29 -> x32, starting transfers between devices: 27.8 us -> 29.6 us  [swap(): return lax.ppermute(array, AXES, list(enumerate(step)))]
    convert_element_type x14 -> x15, other arithmetic: 4.95 us -> 4.08 us  [the longest x4 2.07 us: end(): keep = self.add(self.keep[:half], moved[0]).astype(BF16)]
  transfers between devices with their start and end apart: 29 -> 32, of which waited for: 20 -> 18; matrix products, arithmetic and copies ran while one was open for 4% -> 6% of each run, Pallas kernels for 22% -> 26%
where the time goes in v2:
time: 217 us; the launch traced here: 216 us
  waiting for transfers between devices  99.8 us (46%)
  Pallas kernels  63.5 us (29%)
  starting transfers between devices  29.6 us (14%)
  local copies, waits for them, and re-layouts  11.6 us (5%)
  other arithmetic  10.3 us (5%)
    ppermute x32, waiting for transfers between devices, swap(): return lax.ppermute(array, AXES, list(enumerate(step)))  99.8 us
    pallas_call x9, Pallas kernels, call(): pl.pallas_call(kernel, in_specs=[smem] * len(scalars) + [whole] * len(inp...  63.5 us
    ppermute x32, starting transfers between devices, swap(): return lax.ppermute(array, AXES, list(enumerate(step)))  29.6 us
  transfers between devices with their start and end apart: 32, of which 18 were waited for; matrix products, arithmetic and copies ran while one was open for 6% of the time, Pallas kernels for 26%

profile of v2, /device:TPU:0, one launch (start us, length us, event | category | flops | bytes accessed | tf_op | source)
XLA Modules:
  0.0 216.4 jit_solution(6953632102481746093)
XLA Ops:
  0.7 0.9 copy.40
  1.5 1.0 maximum_bitcast_fusion.1
  2.5 3.1 %collective-permute-start = (bf16[1,96,768]{2,1,0:T(8,128)(2,1)S(1)}, bf16[1,96,768]{2,1,0:T(8,128)(2,1)S(1)}, u32[]{:S(2)}, u32[]{:S(2)}) collective-permute-start(bf16[1,96,768]{2,1,0:T(8,128)(2,1)S(1)} %maximum_bitcast_fusion.1), channel_id=1, source_target_pairs={{0,8},{1,17},{2,10},{3,19},{4,12},{5,21},{6,14},{7,23},{8,0},{9,25... | collective-permute-start | bytes 442376 | tf_op jit(solution)/shard_map/ppermute | solution.py:37
  5.6 0.8 reshape.167
  6.4 0.8 reshape.168
  7.2 1.0 maximum_bitcast_fusion
  8.2 1.7 collective-permute-done
  9.9 2.3 %collective-permute-start.2 = (bf16[1,2,96,768]{3,2,0,1:T(8,128)(2,1)S(1)}, bf16[1,2,96,768]{3,2,0,1:T(8,128)(2,1)S(1)}, u32[]{:S(2)}, u32[]{:S(2)}) collective-permute-start(bf16[1,2,96,768]{3,2,0,1:T(8,128)(2,1)S(1)} %maximum_bitcast_fusion), channel_id=1, source_target_pairs={{0,8},{1,17},{2,10},{3,19},{4,12},{5,21},{6,14},{7,23},{8,0},{9,25... | collective-permute-start | bytes 884744 | tf_op jit(solution)/shard_map/ppermute | solution.py:37
  13.0 1.6 collective-permute-start.1
  14.6 5.4 %collective-permute-done.2 = bf16[1,2,96,768]{3,2,0,1:T(8,128)(2,1)S(1)} collective-permute-done((bf16[1,2,96,768]{3,2,0,1:T(8,128)(2,1)S(1)}, bf16[1,2,96,768]{3,2,0,1:T(8,128)(2,1)S(1)}, u32[]{:S(2)}, u32[]{:S(2)}) %collective-permute-start.2) | collective-permute-done | bytes 294944 | tf_op jit(solution)/shard_map/ppermute | solution.py:37
  20.1 2.4 %collective-permute-start.3 = (bf16[4,96,768]{2,1,0:T(8,128)(2,1)S(1)}, bf16[4,96,768]{2,1,0:T(8,128)(2,1)S(1)}, u32[]{:S(2)}, u32[]{:S(2)}) collective-permute-start(bf16[4,96,768]{2,1,0:T(8,128)(2,1)S(1)} %pad_maximum_fusion.8), channel_id=1, source_target_pairs={{0,16},{1,9},{2,18},{3,11},{4,20},{5,13},{6,22},{7,15},{8,24},{9,1... | collective-permute-start | bytes 1769480 | tf_op jit(solution)/shard_map/ppermute | solution.py:37
  22.5 1.5 collective-permute-start.4
  24.0 13.3 %collective-permute-done.3 = bf16[4,96,768]{2,1,0:T(8,128)(2,1)S(1)} collective-permute-done((bf16[4,96,768]{2,1,0:T(8,128)(2,1)S(1)}, bf16[4,96,768]{2,1,0:T(8,128)(2,1)S(1)}, u32[]{:S(2)}, u32[]{:S(2)}) %collective-permute-start.3) | collective-permute-done | bytes 589856 | tf_op jit(solution)/shard_map/ppermute | solution.py:37
  37.5 1.8 collective-permute-start.5
  39.3 0.9 slice_bitcast_fusion
  40.3 17.1 %collective-permute-done.6 = bf16[4,96,768]{2,1,0:T(8,128)(2,1)S(1)} collective-permute-done((bf16[4,96,768]{2,1,0:T(8,128)(2,1)S(1)}, bf16[4,96,768]{2,1,0:T(8,128)(2,1)S(1)}, u32[]{:S(2)}, u32[]{:S(2)}) %collective-permute-start.6) | collective-permute-done | bytes 589856 | tf_op jit(solution)/shard_map/ppermute | solution.py:37
  60.0 7.4 %shard_map.332 = (bf16[2,768,768]{2,1,0:T(8,128)(2,1)S(1)}, bf16[2,512,576]{2,1,0:T(8,128)(2,1)S(1)}, bf16[2,192,512]{2,1,0:T(8,128)(2,1)S(1)}, bf16[2,3,512,512...) custom-call(s32[32]{0:T(128)S(1)} %fusion.31.place_ref, ...), custom_call_target="tpu_custom_call" | custom-call | flops 1024 | bytes 1024 | tf_op jit(solution)/shard_map/pallas_call | solution.py:428
  67.5 8.7 %shard_map.333 = (bf16[2,768,768]{2,1,0:T(8,128)(2,1)S(1)}, bf16[2,512,576]{2,1,0:T(8,128)(2,1)S(1)}, bf16[2,192,512]{2,1,0:T(8,128)(2,1)S(1)}, bf16[2,3,512,512...) custom-call(s32[32]{0:T(128)S(1)} %fusion.31.place_ref, ...), custom_call_target="tpu_custom_call" | custom-call | flops 1024 | bytes 1024 | tf_op jit(solution)/shard_map/pallas_call | solution.py:428
  76.3 1.0 copy-done.3
  77.4 1.0 collective-permute-start.10
  78.4 1.3 pad_maximum_fusion.5.rest_0_
  79.7 1.2 collective-permute-start.13
  81.7 0.9 collective-permute-done.11.rest_3_
  82.7 6.4 %shard_map.334 = (bf16[2,768,768]{2,1,0:T(8,128)(2,1)S(1)}, bf16[2,512,768]{2,1,0:T(8,128)(2,1)S(1)}, bf16[2,512,768]{2,1,0:T(8,128)(2,1)S(1)}, bf16[2,768,768]{...) custom-call(s32[32]{0:T(128)S(1)} %fusion.31.place_ref, ...), custom_call_target="tpu_custom_call" | custom-call | flops 1024 | bytes 1024 | tf_op jit(solution)/shard_map/pallas_call | solution.py:428
  89.1 6.9 %collective-permute-done.13.rest_1_ = bf16[8,96,768]{2,1,0:T(8,128)(2,1)S(1)} collective-permute-done((bf16[8,96,768]{2,1,0:T(8,128)(2,1)S(1)}, bf16[8,96,768]{2,1,0:T(8,128)(2,1)S(1)}, u32[]{:S(2)}, u32[]{:S(2)}) %collective-permute-start.13) | collective-permute-done | bytes 1179680 | tf_op jit(solution)/shard_map/ppermute | solution.py:37
  97.3 2.5 %shard_map.335 = (bf16[2,768,768]{2,1,0:T(8,128)(2,1)S(1)}, f32[512,768]{1,0:T(8,128)S(1)}) custom-call(s32[32]{0:T(128)S(1)} %fusion.31.place_ref, bf16[2,512,768]{2,1,0:T(8,128)(2,1)S(1)} %get-tuple-element.99.active_ref, f32[512,768]{1,0:T(8,128)S(1)} %get-tuple-element.100.normal_ref.rest_2_, f32[1,768]{1,0:T(1,128)S(1)} %stack.50.rest_1_.first_gain.rest_4_, ...), custom_call_target="tpu_custom_call" | custom-call | flops 1024 | bytes 1024 | tf_op jit(solution)/shard_map/pallas_call | solution.py:428
  99.8 0.8 collective-permute-done.15.rest_1_
  100.5 6.6 %shard_map.336 = (bf16[2,768,768]{2,1,0:T(8,128)(2,1)S(1)}, f32[512,768]{1,0:T(8,128)}, f32[512,768]{1,0:T(8,128)S(1)}, bf16[512,768]{1,0:T(8,128)(2,1)S(1)}, bf...) custom-call(s32[32]{0:T(128)S(1)} %fusion.31.place_ref, ...), custom_call_target="tpu_custom_call" | custom-call | flops 1024 | bytes 1024 | tf_op jit(solution)/shard_map/pallas_call | solution.py:428
  107.9 2.1 shard_map.337
  110.3 1.7 collective-permute-done.16
  112.6 1.2 collective-permute-start.20
  113.9 5.1 %shard_map.338 = (bf16[16,96,768]{2,1,0:T(8,128)(2,1)S(1)}, f32[8,768]{1,0:T(8,128)S(1)}, f32[512,768]{1,0:T(8,128)S(1)}, bf16[768,512]{1,0:T(8,128)(2,1)S(1)}) custom-call(s32[32]{0:T(128)S(1)} %fusion.32.slot_ref, bf16[512,768]{1,0:T(8,128)(2,1)S(1)} %get-tuple-element.112.low_grad_ref, bf16[2,512,768]{2,1,0:T(8,128)(2,1)S(1)} %get-tuple-element.104.slope_ref, ...), custom_call_target="tpu_custom_call" | custom-call | flops 1024 | bytes 1024 | tf_op jit(solution)/shard_map/pallas_call | solution.py:428
  119.7 5.8 %shard_map.339 = (bf16[16,96,768]{2,1,0:T(8,128)(2,1)S(1)}, f32[8,768]{1,0:T(8,128)S(1)}, f32[512,768]{1,0:T(8,128)S(1)}, bf16[512,768]{1,0:T(8,128)(2,1)S(1)}, bf16[768,512]{1,0:T(8,128)(2,1)S(1)}) custom-call(s32[32]{0:T(128)S(1)} %fusion.32.slot_ref, bf16[512,768]{1,0:T(8,128)(2,1)S(1)} %get-tuple-element.112.low_grad_ref, ...), custom_call_target="tpu_custom_call" | custom-call | flops 1024 | bytes 1024 | tf_op jit(solution)/shard_map/pallas_call | solution.py:428
  125.5 3.4 %collective-permute-done.20 = bf16[8,96,768]{2,1,0:T(8,128)(2,1)S(1)} collective-permute-done((bf16[8,96,768]{2,1,0:T(8,128)(2,1)S(1)}, bf16[8,96,768]{2,1,0:T(8,128)(2,1)S(1)}, u32[]{:S(2)}, u32[]{:S(2)}) %collective-permute-start.20) | collective-permute-done | bytes 1179680 | tf_op jit(solution)/shard_map/ppermute | solution.py:37
  130.1 1.2 collective-permute-start.22
  131.3 2.9 %collective-permute-start.21 = (bf16[4,96,768]{2,1,0:T(8,128)(2,1)S(1)}, bf16[4,96,768]{2,1,0:T(8,128)(2,1)S(1)}, u32[]{:S(2)}, u32[]{:S(2)}) collective-permute-start(bf16[4,96,768]{2,1,0:T(8,128)(2,1)S(1)} %get-tuple-element.144), channel_id=1, source_target_pairs={{0,16},{1,9},{2,18},{3,11},{4,20},{5,13},{6,22},{7,15},{8,24},{9,1... | collective-permute-start | bytes 1769480 | tf_op jit(solution)/shard_map/ppermute | solution.py:37
  134.4 18.8 %shard_map.340 = (f32[512,768]{1,0:T(8,128)}, f32[2,8,768]{2,1,0:T(8,128)}, f32[2,8,768]{2,1,0:T(8,128)}, bf16[16,112,768]{2,1,0:T(8,128)(2,1)S(1)}, bf16[16,112,768]{2,1,0:T(8,128)(2,1)S(1)}) custom-call(s32[32]{0:T(128)S(1)} %fusion.32.slot_ref, bf16[768,512]{1,0:T(8,128)(2,1)S(1)} %copy-done.7, f32[512,768]{1,0:T(8,128)S(1)} %get-tuple-element.121.resid_ref, ...), custom_call_target="tpu_custom_call" | custom-call | flops 1024 | bytes 1024 | tf_op jit(solution)/shard_map/pallas_call | solution.py:428
  154.6 2.0 collective-permute-done.24
  159.7 15.6 %collective-permute-done.26 = bf16[4,96,768]{2,1,0:T(8,128)(2,1)S(1)} collective-permute-done((bf16[4,96,768]{2,1,0:T(8,128)(2,1)S(1)}, bf16[4,96,768]{2,1,0:T(8,128)(2,1)S(1)}, u32[]{:S(2)}, u32[]{:S(2)}) %collective-permute-start.26) | collective-permute-done | bytes 589856 | tf_op jit(solution)/shard_map/ppermute | solution.py:37
  177.2 1.6 collective-permute-start.28
  179.0 8.2 %collective-permute-done.28 = bf16[2,2,96,768]{3,2,0,1:T(8,128)(2,1)S(1)} collective-permute-done((bf16[2,2,96,768]{3,2,0,1:T(8,128)(2,1)S(1)}, bf16[2,2,96,768]{3,2,0,1:T(8,128)(2,1)S(1)}, u32[]{:S(2)}, u32[]{:S(2)}) %collective-permute-start.28) | collective-permute-done | bytes 589856 | tf_op jit(solution)/shard_map/ppermute | solution.py:37
  187.2 12.4 %collective-permute-done.27 = bf16[4,112,768]{2,1,0:T(8,128)(2,1)S(1)} collective-permute-done((bf16[4,112,768]{2,1,0:T(8,128)(2,1)S(1)}, bf16[4,112,768]{2,1,0:T(8,128)(2,1)S(1)}, u32[]{:S(2)}, u32[]{:S(2)}) %collective-permute-start.27) | collective-permute-done | bytes 688160 | tf_op jit(solution)/shard_map/ppermute | solution.py:37
  200.1 1.6 collective-permute-start.29
  201.8 5.1 %collective-permute-done.31 = bf16[1,2,96,768]{3,2,0,1:T(8,128)(2,1)S(1)} collective-permute-done((bf16[1,2,96,768]{3,2,0,1:T(8,128)(2,1)S(1)}, bf16[1,2,96,768]{3,2,0,1:T(8,128)(2,1)S(1)}, u32[]{:S(2)}, u32[]{:S(2)}) %collective-permute-start.31) | collective-permute-done | bytes 294944 | tf_op jit(solution)/shard_map/ppermute | solution.py:37
  207.0 0.8 slice_bitcast_fusion.2
  208.1 1.6 collective-permute-start.30
  209.8 3.8 %collective-permute-done.30 = bf16[1,112,768]{2,1,0:T(8,128)(2,1)S(1)} collective-permute-done((bf16[1,112,768]{2,1,0:T(8,128)(2,1)S(1)}, bf16[1,112,768]{2,1,0:T(8,128)(2,1)S(1)}, u32[]{:S(2)}, u32[]{:S(2)}) %collective-permute-start.30) | collective-permute-done | bytes 172064 | tf_op jit(solution)/shard_map/ppermute | solution.py:37
  214.9 0.8 slice_bitcast_fusion.4
  (158 shorter events, 18.9 us)
Async XLA Ops:
  2.5 7.4 %collective-permute-start = (bf16[1,96,768]{2,1,0:T(8,128)(2,1)S(1)}, bf16[1,96,768]{2,1,0:T(8,128)(2,1)S(1)}, u32[]{:S(2)}, u32[]{:S(2)}) collective-permute-start(bf16[1,96,768]{2,1,0:T(8,128)(2,1)S(1)} %maximum_bitcast_fusion.1), channel_id=1, source_target_pairs={{0,8},{1,17},{2,10},{3,19},{4,12},{5,21},{6,14},{7,23},{8,0},{9,25... | collective-permute-start | bytes 442376 | tf_op jit(solution)/shard_map/ppermute | solution.py:37
  9.9 10.0 %collective-permute-start.2 = (bf16[1,2,96,768]{3,2,0,1:T(8,128)(2,1)S(1)}, bf16[1,2,96,768]{3,2,0,1:T(8,128)(2,1)S(1)}, u32[]{:S(2)}, u32[]{:S(2)}) collective-permute-start(bf16[1,2,96,768]{3,2,0,1:T(8,128)(2,1)S(1)} %maximum_bitcast_fusion), channel_id=1, source_target_pairs={{0,8},{1,17},{2,10},{3,19},{4,12},{5,21},{6,14},{7,23},{8,0},{9,25... | collective-permute-start | bytes 884744 | tf_op jit(solution)/shard_map/ppermute | solution.py:37
  13.0 7.0 %collective-permute-start.1 = (bf16[2,96,768]{2,1,0:T(8,128)(2,1)S(1)}, bf16[2,96,768]{2,1,0:T(8,128)(2,1)S(1)}, u32[]{:S(2)}, u32[]{:S(2)}) collective-permute-start(bf16[2,96,768]{2,1,0:T(8,128)(2,1)S(1)} %pad_maximum_fusion.14), channel_id=1, source_target_pairs={{0,4},{1,3},{2,6},{3,1},{4,0},{5,7},{6,2},{7,5},{8,12},{9,11},{10,... | collective-permute-start | bytes 884744 | tf_op jit(solution)/shard_map/ppermute | solution.py:37
  20.1 17.2 %collective-permute-start.3 = (bf16[4,96,768]{2,1,0:T(8,128)(2,1)S(1)}, bf16[4,96,768]{2,1,0:T(8,128)(2,1)S(1)}, u32[]{:S(2)}, u32[]{:S(2)}) collective-permute-start(bf16[4,96,768]{2,1,0:T(8,128)(2,1)S(1)} %pad_maximum_fusion.8), channel_id=1, source_target_pairs={{0,16},{1,9},{2,18},{3,11},{4,20},{5,13},{6,22},{7,15},{8,24},{9,1... | collective-permute-start | bytes 1769480 | tf_op jit(solution)/shard_map/ppermute | solution.py:37
  22.5 14.9 %collective-permute-start.4 = (bf16[2,2,96,768]{3,2,0,1:T(8,128)(2,1)S(1)}, bf16[2,2,96,768]{3,2,0,1:T(8,128)(2,1)S(1)}, u32[]{:S(2)}, u32[]{:S(2)}) collective-permute-start(bf16[2,2,96,768]{3,2,0,1:T(8,128)(2,1)S(1)} %pad_maximum_fusion.9), channel_id=1, source_target_pairs={{0,4},{1,3},{2,6},{3,1},{4,0},{5,7},{6,2},{7,5},{8,12},{9,11},{10,... | collective-permute-start | bytes 1769480 | tf_op jit(solution)/shard_map/ppermute | solution.py:37
  37.5 19.9 %collective-permute-start.5 = (bf16[8,96,768]{2,1,0:T(8,128)(2,1)S(1)}, bf16[8,96,768]{2,1,0:T(8,128)(2,1)}, u32[]{:S(2)}, u32[]{:S(2)}) collective-permute-start(bf16[8,96,768]{2,1,0:T(8,128)(2,1)S(1)} %pad_maximum_fusion.2.rest_1_), channel_id=1, source_target_pairs={{0,2},{1,5},{2,0},{3,7},{4,6},{5,1},{6,4},{7,3},{8,10},{9,13},{10,... | collective-permute-start | bytes 3538952 | tf_op jit(solution)/shard_map/ppermute | solution.py:37
  40.2 18.4 %copy-start.13 = (f32[768]{0:T(1024)S(1)}, f32[768]{0:T(1024)}, u32[]{:S(2)}) copy-start(f32[768]{0:T(1024)} %param.30) | copy-start | bytes 9220
  40.2 18.4 %copy-start.14 = (f32[768]{0:T(1024)S(1)}, f32[768]{0:T(1024)}, u32[]{:S(2)}) copy-start(f32[768]{0:T(1024)} %param.31) | copy-start | bytes 9220
  40.2 18.4 %copy-start.15 = (f32[768]{0:T(1024)S(1)}, f32[768]{0:T(1024)}, u32[]{:S(2)}) copy-start(f32[768]{0:T(1024)} %param.29) | copy-start | bytes 9220
  40.2 19.8 %copy-start = (bf16[512,768]{1,0:T(8,128)(2,1)S(1)}, bf16[512,768]{1,0:T(8,128)(2,1)}, u32[]{:S(2)}) copy-start(bf16[512,768]{1,0:T(8,128)(2,1)} %tokens_ref.3) | copy-start | bytes 2359300
  40.2 17.2 %collective-permute-start.6 = (bf16[4,96,768]{2,1,0:T(8,128)(2,1)S(1)}, bf16[4,96,768]{2,1,0:T(8,128)(2,1)S(1)}, u32[]{:S(2)}, u32[]{:S(2)}) collective-permute-start(bf16[4,96,768]{2,1,0:T(8,128)(2,1)S(1)} %get-tuple-element.233), channel_id=1, source_target_pairs={{0,16},{1,9},{2,18},{3,11},{4,20},{5,13},{6,22},{7,15},{8,24},{9,1... | collective-permute-start | bytes 1769480 | tf_op jit(solution)/shard_map/ppermute | solution.py:37
  57.5 10.0 %collective-permute-start.7 = (bf16[8,96,768]{2,1,0:T(8,128)(2,1)S(1)}, bf16[8,96,768]{2,1,0:T(8,128)(2,1)}, u32[]{:S(2)}, u32[]{:S(2)}) collective-permute-start(bf16[8,96,768]{2,1,0:T(8,128)(2,1)S(1)} %pad_maximum_fusion.2.rest_1_), channel_id=1, source_target_pairs={{0,1},{1,0},{2,3},{3,2},{4,5},{5,4},{6,7},{7,6},{8,9},{9,8},{10,11... | collective-permute-start | bytes 3538952 | tf_op jit(solution)/shard_map/ppermute | solution.py:37
  57.6 9.9 %collective-permute-start.8 = (bf16[8,96,768]{2,1,0:T(8,128)(2,1)}, bf16[8,96,768]{2,1,0:T(8,128)(2,1)}, u32[]{:S(2)}, u32[]{:S(2)}) collective-permute-start(bf16[8,96,768]{2,1,0:T(8,128)(2,1)} %collective-permute-done.5.rest_2_), channel_id=1, source_target_pairs={{0,1},{1,0},{2,3},{3,2},{4,5},{5,4},{6,7},{7,6},{8,9},{9,8},{10,11... | collective-permute-start | bytes 3538952 | tf_op jit(solution)/shard_map/ppermute | solution.py:37
  58.1 19.3 %collective-permute-start.9 = (bf16[8,96,768]{2,1,0:T(8,128)(2,1)S(1)}, bf16[8,96,768]{2,1,0:T(8,128)(2,1)}, u32[]{:S(2)}, u32[]{:S(2)}) collective-permute-start(bf16[8,96,768]{2,1,0:T(8,128)(2,1)S(1)} %pad_maximum_fusion.4.rest_0_), channel_id=1, source_target_pairs={{0,2},{1,5},{2,0},{3,7},{4,6},{5,1},{6,4},{7,3},{8,10},{9,13},{10,... | collective-permute-start | bytes 3538952 | tf_op jit(solution)/shard_map/ppermute | solution.py:37
  58.4 20.0 %collective-permute-start.12 = (bf16[4,96,768]{2,1,0:T(8,128)(2,1)}, bf16[4,96,768]{2,1,0:T(8,128)(2,1)}, u32[]{:S(2)}, u32[]{:S(2)}) collective-permute-start(bf16[4,96,768]{2,1,0:T(8,128)(2,1)} %get-tuple-element.101), channel_id=1, source_target_pairs={{0,16},{1,9},{2,18},{3,11},{4,20},{5,13},{6,22},{7,15},{8,24},{9,1... | collective-permute-start | bytes 1769480 | tf_op jit(solution)/shard_map/ppermute | solution.py:37
  67.5 8.8 %copy-start.1 = (bf16[2,512,576]{2,1,0:T(8,128)(2,1)}, bf16[2,512,576]{2,1,0:T(8,128)(2,1)S(1)}, u32[]{:S(2)}) copy-start(bf16[2,512,576]{2,1,0:T(8,128)(2,1)S(1)} %get-tuple-element.136.rest_7_) | copy-start | bytes 3538948
  67.5 8.8 %copy-start.6 = (bf16[768,512]{1,0:T(8,128)(2,1)}, bf16[768,512]{1,0:T(8,128)(2,1)S(1)}, u32[]{:S(2)}) copy-start(bf16[768,512]{1,0:T(8,128)(2,1)S(1)} %get-tuple-element.108.turned_ref) | copy-start | bytes 2359300
  67.5 8.8 %copy-start.8 = (bf16[2,192,512]{2,1,0:T(8,128)(2,1)}, bf16[2,192,512]{2,1,0:T(8,128)(2,1)S(1)}, u32[]{:S(2)}) copy-start(bf16[2,192,512]{2,1,0:T(8,128)(2,1)S(1)} %get-tuple-element.137.rest_8_) | copy-start | bytes 1179652
  77.4 11.8 %copy-start.10 = (bf16[2,192,512]{2,1,0:T(8,128)(2,1)}, bf16[2,192,512]{2,1,0:T(8,128)(2,1)S(1)}, u32[]{:S(2)}) copy-start(bf16[2,192,512]{2,1,0:T(8,128)(2,1)S(1)} %get-tuple-element.132.rest_2_) | copy-start | bytes 1179652
  77.4 5.3 %copy-start.12 = (f32[3072]{0:T(1024)S(1)}, f32[3072]{0:T(1024)}, u32[]{:S(2)}) copy-start(f32[3072]{0:T(1024)} %param.33) | copy-start | bytes 36868
  77.4 4.4 %collective-permute-start.10 = (bf16[8,96,768]{2,1,0:T(8,128)(2,1)S(1)}, bf16[8,96,768]{2,1,0:T(8,128)(2,1)S(1)}, u32[]{:S(2)}, u32[]{:S(2)}) collective-permute-start(bf16[8,96,768]{2,1,0:T(8,128)(2,1)S(1)} %pad_maximum_fusion.4.rest_0_), channel_id=1, source_target_pairs={{0,1},{1,0},{2,3},{3,2},{4,5},{5,4},{6,7},{7,6},{8,9},{9,8},{10,11... | collective-permute-start | bytes 3538952 | tf_op jit(solution)/shard_map/ppermute | solution.py:37
  78.3 4.4 %collective-permute-start.11 = (bf16[8,96,768]{2,1,0:T(8,128)(2,1)}, bf16[8,96,768]{2,1,0:T(8,128)(2,1)S(1)}, u32[]{:S(2)}, u32[]{:S(2)}) collective-permute-start(bf16[8,96,768]{2,1,0:T(8,128)(2,1)} %collective-permute-done.9.rest_1_), channel_id=1, source_target_pairs={{0,1},{1,0},{2,3},{3,2},{4,5},{5,4},{6,7},{7,6},{8,9},{9,8},{10,11... | collective-permute-start | bytes 3538952 | tf_op jit(solution)/shard_map/ppermute | solution.py:37
  79.7 16.3 %collective-permute-start.13 = (bf16[8,96,768]{2,1,0:T(8,128)(2,1)S(1)}, bf16[8,96,768]{2,1,0:T(8,128)(2,1)S(1)}, u32[]{:S(2)}, u32[]{:S(2)}) collective-permute-start(bf16[8,96,768]{2,1,0:T(8,128)(2,1)S(1)} %pad_maximum_fusion.5.rest_0_), channel_id=1, source_target_pairs={{0,2},{1,5},{2,0},{3,7},{4,6},{5,1},{6,4},{7,3},{8,10},{9,13},{10,... | collective-permute-start | bytes 3538952 | tf_op jit(solution)/shard_map/ppermute | solution.py:37
  82.7 13.8 %copy-start.16 = (f32[768]{0:T(1024)S(1)}, f32[768]{0:T(1024)}, u32[]{:S(2)}) copy-start(f32[768]{0:T(1024)} %param.35) | copy-start | bytes 9220
  82.7 13.8 %copy-start.17 = (f32[768]{0:T(1024)S(1)}, f32[768]{0:T(1024)}, u32[]{:S(2)}) copy-start(f32[768]{0:T(1024)} %param.36) | copy-start | bytes 9220
  82.7 13.9 %copy-start.18 = (f32[768]{0:T(1024)S(1)}, f32[768]{0:T(1024)}, u32[]{:S(2)}) copy-start(f32[768]{0:T(1024)} %param.37) | copy-start | bytes 9220
  96.0 3.8 %collective-permute-start.14 = (bf16[8,96,768]{2,1,0:T(8,128)(2,1)S(1)}, bf16[8,96,768]{2,1,0:T(8,128)(2,1)S(1)}, u32[]{:S(2)}, u32[]{:S(2)}) collective-permute-start(bf16[8,96,768]{2,1,0:T(8,128)(2,1)S(1)} %pad_maximum_fusion.5.rest_0_), channel_id=1, source_target_pairs={{0,1},{1,0},{2,3},{3,2},{4,5},{5,4},{6,7},{7,6},{8,9},{9,8},{10,11... | collective-permute-start | bytes 3538952 | tf_op jit(solution)/shard_map/ppermute | solution.py:37
  96.0 4.5 %collective-permute-start.15 = (bf16[8,96,768]{2,1,0:T(8,128)(2,1)S(1)}, bf16[8,96,768]{2,1,0:T(8,128)(2,1)S(1)}, u32[]{:S(2)}, u32[]{:S(2)}) collective-permute-start(bf16[8,96,768]{2,1,0:T(8,128)(2,1)S(1)} %collective-permute-done.13.rest_1_), channel_id=1, source_target_pairs={{0,1},{1,0},{2,3},{3,2},{4,5},{5,4},{6,7},{7,6},{8,9},{9,8},{10,11... | collective-permute-start | bytes 3538952 | tf_op jit(solution)/shard_map/ppermute | solution.py:37
  107.3 2.9 %collective-permute-start.19 = (bf16[8,96,768]{2,1,0:T(8,128)(2,1)S(1)}, bf16[8,96,768]{2,1,0:T(8,128)(2,1)S(1)}, u32[]{:S(2)}, u32[]{:S(2)}) collective-permute-start(bf16[8,96,768]{2,1,0:T(8,128)(2,1)S(1)} %get-tuple-element.220), channel_id=1, source_target_pairs={{0,1},{1,0},{2,3},{3,2},{4,5},{5,4},{6,7},{7,6},{8,9},{9,8},{10,11... | collective-permute-start | bytes 3538952 | tf_op jit(solution)/shard_map/ppermute | solution.py:37
  107.6 4.4 %collective-permute-start.16 = (bf16[8,96,768]{2,1,0:T(8,128)(2,1)S(1)}, bf16[8,96,768]{2,1,0:T(8,128)(2,1)S(1)}, u32[]{:S(2)}, u32[]{:S(2)}) collective-permute-start(bf16[8,96,768]{2,1,0:T(8,128)(2,1)S(1)} %get-tuple-element.221), channel_id=1, source_target_pairs={{0,1},{1,0},{2,3},{3,2},{4,5},{5,4},{6,7},{7,6},{8,9},{9,8},{10,11... | collective-permute-start | bytes 3538952 | tf_op jit(solution)/shard_map/ppermute | solution.py:37
  112.6 16.3 %collective-permute-start.20 = (bf16[8,96,768]{2,1,0:T(8,128)(2,1)S(1)}, bf16[8,96,768]{2,1,0:T(8,128)(2,1)S(1)}, u32[]{:S(2)}, u32[]{:S(2)}) collective-permute-start(bf16[8,96,768]{2,1,0:T(8,128)(2,1)S(1)} %get-tuple-element.219), channel_id=1, source_target_pairs={{0,2},{1,5},{2,0},{3,7},{4,6},{5,1},{6,4},{7,3},{8,10},{9,13},{10,... | collective-permute-start | bytes 3538952 | tf_op jit(solution)/shard_map/ppermute | solution.py:37
  119.1 10.1 %collective-permute-start.18 = (bf16[8,96,768]{2,1,0:T(8,128)(2,1)S(1)}, bf16[8,96,768]{2,1,0:T(8,128)(2,1)S(1)}, u32[]{:S(2)}, u32[]{:S(2)}) collective-permute-start(bf16[8,96,768]{2,1,0:T(8,128)(2,1)S(1)} %get-tuple-element.222), channel_id=1, source_target_pairs={{0,1},{1,0},{2,3},{3,2},{4,5},{5,4},{6,7},{7,6},{8,9},{9,8},{10,11... | collective-permute-start | bytes 3538952 | tf_op jit(solution)/shard_map/ppermute | solution.py:37
  119.2 10.0 %collective-permute-start.17 = (bf16[8,96,768]{2,1,0:T(8,128)(2,1)S(1)}, bf16[8,96,768]{2,1,0:T(8,128)(2,1)S(1)}, u32[]{:S(2)}, u32[]{:S(2)}) collective-permute-start(bf16[8,96,768]{2,1,0:T(8,128)(2,1)S(1)} %get-tuple-element.223), channel_id=1, source_target_pairs={{0,1},{1,0},{2,3},{3,2},{4,5},{5,4},{6,7},{7,6},{8,9},{9,8},{10,11... | collective-permute-start | bytes 3538952 | tf_op jit(solution)/shard_map/ppermute | solution.py:37
  129.3 5.1 %copy-start.2 = (bf16[2,512,576]{2,1,0:T(8,128)(2,1)S(1)}, bf16[2,512,576]{2,1,0:T(8,128)(2,1)}, u32[]{:S(2)}) copy-start(bf16[2,512,576]{2,1,0:T(8,128)(2,1)} %copy-done.1) | copy-start | bytes 3538948
  129.3 5.1 %copy-start.4 = (bf16[2,512,576]{2,1,0:T(8,128)(2,1)S(1)}, bf16[2,512,576]{2,1,0:T(8,128)(2,1)}, u32[]{:S(2)}) copy-start(bf16[2,512,576]{2,1,0:T(8,128)(2,1)} %copy-done.3) | copy-start | bytes 3538948
  129.3 5.1 %copy-start.7 = (bf16[768,512]{1,0:T(8,128)(2,1)S(1)}, bf16[768,512]{1,0:T(8,128)(2,1)}, u32[]{:S(2)}) copy-start(bf16[768,512]{1,0:T(8,128)(2,1)} %copy-done.6) | copy-start | bytes 2359300
  129.3 5.1 %copy-start.9 = (bf16[2,192,512]{2,1,0:T(8,128)(2,1)S(1)}, bf16[2,192,512]{2,1,0:T(8,128)(2,1)}, u32[]{:S(2)}) copy-start(bf16[2,192,512]{2,1,0:T(8,128)(2,1)} %copy-done.8) | copy-start | bytes 1179652
  130.1 23.1 %collective-permute-start.22 = (bf16[8,96,768]{2,1,0:T(8,128)(2,1)S(1)}, bf16[8,96,768]{2,1,0:T(8,128)(2,1)S(1)}, u32[]{:S(2)}, u32[]{:S(2)}) collective-permute-start(bf16[8,96,768]{2,1,0:T(8,128)(2,1)S(1)} %get-tuple-element.217), channel_id=1, source_target_pairs={{0,2},{1,5},{2,0},{3,7},{4,6},{5,1},{6,4},{7,3},{8,10},{9,13},{10,... | collective-permute-start | bytes 3538952 | tf_op jit(solution)/shard_map/ppermute | solution.py:37
  131.3 21.9 %collective-permute-start.21 = (bf16[4,96,768]{2,1,0:T(8,128)(2,1)S(1)}, bf16[4,96,768]{2,1,0:T(8,128)(2,1)S(1)}, u32[]{:S(2)}, u32[]{:S(2)}) collective-permute-start(bf16[4,96,768]{2,1,0:T(8,128)(2,1)S(1)} %get-tuple-element.144), channel_id=1, source_target_pairs={{0,16},{1,9},{2,18},{3,11},{4,20},{5,13},{6,22},{7,15},{8,24},{9,1... | collective-permute-start | bytes 1769480 | tf_op jit(solution)/shard_map/ppermute | solution.py:37
  153.4 3.2 %collective-permute-start.24 = (bf16[8,112,768]{2,1,0:T(8,128)(2,1)S(1)}, bf16[8,112,768]{2,1,0:T(8,128)(2,1)S(1)}, u32[]{:S(2)}, u32[]{:S(2)}) collective-permute-start(bf16[8,112,768]{2,1,0:T(8,128)(2,1)S(1)} %get-tuple-element.211), channel_id=1, source_target_pairs={{0,1},{1,0},{2,3},{3,2},{4,5},{5,4},{6,7},{7,6},{8,9},{9,8},{10,11... | collective-permute-start | bytes 4128776 | tf_op jit(solution)/shard_map/ppermute | solution.py:37
  154.0 4.9 %collective-permute-start.23 = (bf16[8,112,768]{2,1,0:T(8,128)(2,1)S(1)}, bf16[8,112,768]{2,1,0:T(8,128)(2,1)S(1)}, u32[]{:S(2)}, u32[]{:S(2)}) collective-permute-start(bf16[8,112,768]{2,1,0:T(8,128)(2,1)S(1)} %get-tuple-element.210), channel_id=1, source_target_pairs={{0,1},{1,0},{2,3},{3,2},{4,5},{5,4},{6,7},{7,6},{8,9},{9,8},{10,11... | collective-permute-start | bytes 4128776 | tf_op jit(solution)/shard_map/ppermute | solution.py:37
  157.4 18.4 %collective-permute-start.25 = (bf16[8,112,768]{2,1,0:T(8,128)(2,1)S(1)}, bf16[8,112,768]{2,1,0:T(8,128)(2,1)S(1)}, u32[]{:S(2)}, u32[]{:S(2)}) collective-permute-start(bf16[8,112,768]{2,1,0:T(8,128)(2,1)S(1)} %pad_maximum_fusion.1), channel_id=1, source_target_pairs={{0,2},{1,5},{2,0},{3,7},{4,6},{5,1},{6,4},{7,3},{8,10},{9,13},{10,... | collective-permute-start | bytes 4128776 | tf_op jit(solution)/shard_map/ppermute | solution.py:37
  158.2 17.1 %collective-permute-start.26 = (bf16[4,96,768]{2,1,0:T(8,128)(2,1)S(1)}, bf16[4,96,768]{2,1,0:T(8,128)(2,1)S(1)}, u32[]{:S(2)}, u32[]{:S(2)}) collective-permute-start(bf16[4,96,768]{2,1,0:T(8,128)(2,1)S(1)} %get-tuple-element.215), channel_id=1, source_target_pairs={{0,16},{1,9},{2,18},{3,11},{4,20},{5,13},{6,22},{7,15},{8,24},{9,1... | collective-permute-start | bytes 1769480 | tf_op jit(solution)/shard_map/ppermute | solution.py:37
  176.8 22.8 %collective-permute-start.27 = (bf16[4,112,768]{2,1,0:T(8,128)(2,1)S(1)}, bf16[4,112,768]{2,1,0:T(8,128)(2,1)S(1)}, u32[]{:S(2)}, u32[]{:S(2)}) collective-permute-start(bf16[4,112,768]{2,1,0:T(8,128)(2,1)S(1)} %pad_maximum_fusion.7), channel_id=1, source_target_pairs={{0,16},{1,9},{2,18},{3,11},{4,20},{5,13},{6,22},{7,15},{8,24},{9,1... | collective-permute-start | bytes 2064392 | tf_op jit(solution)/shard_map/ppermute | solution.py:37
  177.2 9.9 %collective-permute-start.28 = (bf16[2,2,96,768]{3,2,0,1:T(8,128)(2,1)S(1)}, bf16[2,2,96,768]{3,2,0,1:T(8,128)(2,1)S(1)}, u32[]{:S(2)}, u32[]{:S(2)}) collective-permute-start(bf16[2,2,96,768]{3,2,0,1:T(8,128)(2,1)S(1)} %pad_maximum_fusion.10), channel_id=1, source_target_pairs={{0,4},{1,3},{2,6},{3,1},{4,0},{5,7},{6,2},{7,5},{8,12},{9,11},{10,... | collective-permute-start | bytes 1769480 | tf_op jit(solution)/shard_map/ppermute | solution.py:37
  200.0 6.9 %collective-permute-start.31 = (bf16[1,2,96,768]{3,2,0,1:T(8,128)(2,1)S(1)}, bf16[1,2,96,768]{3,2,0,1:T(8,128)(2,1)S(1)}, u32[]{:S(2)}, u32[]{:S(2)}) collective-permute-start(bf16[1,2,96,768]{3,2,0,1:T(8,128)(2,1)S(1)} %add_convert_fusion.8), channel_id=1, source_target_pairs={{0,8},{1,17},{2,10},{3,19},{4,12},{5,21},{6,14},{7,23},{8,0},{9,25... | collective-permute-start | bytes 884744 | tf_op jit(solution)/shard_map/ppermute | solution.py:37
  200.1 7.7 %collective-permute-start.29 = (bf16[2,112,768]{2,1,0:T(8,128)(2,1)S(1)}, bf16[2,112,768]{2,1,0:T(8,128)(2,1)S(1)}, u32[]{:S(2)}, u32[]{:S(2)}) collective-permute-start(bf16[2,112,768]{2,1,0:T(8,128)(2,1)S(1)} %pad_maximum_fusion.12), channel_id=1, source_target_pairs={{0,4},{1,3},{2,6},{3,1},{4,0},{5,7},{6,2},{7,5},{8,12},{9,11},{10,... | collective-permute-start | bytes 1032200 | tf_op jit(solution)/shard_map/ppermute | solution.py:37
  208.1 5.5 %collective-permute-start.30 = (bf16[1,112,768]{2,1,0:T(8,128)(2,1)S(1)}, bf16[1,112,768]{2,1,0:T(8,128)(2,1)S(1)}, u32[]{:S(2)}, u32[]{:S(2)}) collective-permute-start(bf16[1,112,768]{2,1,0:T(8,128)(2,1)S(1)} %pad_maximum_fusion.15), channel_id=1, source_target_pairs={{0,8},{1,17},{2,10},{3,19},{4,12},{5,21},{6,14},{7,23},{8,0},{9,25... | collective-permute-start | bytes 516104 | tf_op jit(solution)/shard_map/ppermute | solution.py:37
  (3 other events, 9.4 us)
